TPU v7x, 32 devices: a whole 2x2x4 slice. The times are simulated.
32 devices in a mesh: tm: 4 (over z), sx: 2 (over core), sy: 4 (over y, x).
Axes of the slice: x: 2, y: 2, z: 4, core: 2. Of those that a mesh axis runs over, the one named last changes fastest.
Arguments:
- initial: float32 [2, 4, 5, 64, 128], P('sx', 'sy'), may hold values from -6 to 6
- viscosity: float32 [2, 4, 128], P('sx', 'sy'), may hold values from 0.5 to 5
- flux_jacobian: float32 [3, 5, 5], replicated, may hold values from -2 to 2
Outputs:
- nodes: float32 [4, 3, 2, 4, 5, 64, 128], P('tm', None, 'sx', 'sy')
All inputs are finite; a program needn't handle non-finite values.
Results may differ from a plain program's by a relative error of at most 0.0001.
Values sent between devices are 32-bit elements; how exact they have to be, the bound alone decides.
No kernel may reach another device: no remote copies, remote signals or barrier semaphores. Data moves between devices by JAX's collectives and lax.ppermute only.
A program may use at most 64 MiB of HBM per device.

v0:
```python
import math

import jax
import jax.numpy as jnp
import numpy as np
from jax import lax
from jax.experimental import pallas as pl
from jax.experimental.pallas import tpu as pltpu
from jax.sharding import PartitionSpec as P

ITERS = 2
JF = 3
JC = 2


SIGMA = 3.0
BETA = 0.5
STEP = 0.1
HALF_STEP = 0.05
TWO_THIRDS = 2.0 / 3.0
ONE_THIRD = 1.0 / 3.0
HIGHEST = lax.Precision.HIGHEST
WEIGHTS = ((5.0 / 24.0, 1.0 / 3.0, -1.0 / 24.0), (-1.0 / 24.0, 1.0 / 3.0, 5.0 / 24.0))


def passed_along(block, axis, distance):
    devices = range(lax.axis_size(axis))
    route = [(i - distance, i) for i in devices if i - distance in devices]
    return lax.ppermute(block, axis, route)


def kron_three(first, second, third):
    return jnp.kron(jnp.kron(first, second), third)


def node_tables():
    places = jnp.arange(4)
    row = places[:, None]
    column = places[None, :]
    identity = (row == column).astype(jnp.float32)
    upper = (row + 1 == column).astype(jnp.float32)
    border = identity * ((row == 0) | (row == 3)).astype(jnp.float32)
    line_laplace = 2.0 * identity - upper - upper.T - border
    line_grad = 0.5 * upper - 0.5 * upper.T
    laplace = (
        kron_three(line_laplace, identity, identity)
        + kron_three(identity, line_laplace, identity)
        + kron_three(identity, identity, line_laplace)
        + SIGMA * jnp.eye(64, dtype=jnp.float32)
    )
    grads = jnp.stack(
        [
            kron_three(line_grad, identity, identity),
            kron_three(identity, line_grad, identity),
            kron_three(identity, identity, line_grad),
        ]
    )
    weighting = jnp.where(row == 0, 0.5, math.sqrt(0.5)).astype(jnp.float32)
    cosine = weighting * jnp.cos(
        math.pi * row.astype(jnp.float32) * (2.0 * column.astype(jnp.float32) + 1.0) / 8.0
    )
    basis = kron_three(cosine, cosine, cosine)
    line_eigen = 2.0 - 2.0 * jnp.cos(math.pi * places.astype(jnp.float32) / 4.0)
    spectrum = (
        line_eigen[:, None, None] + line_eigen[None, :, None] + line_eigen[None, None, :]
    ).reshape(64) + SIGMA
    return (laplace, grads, basis, spectrum)


def previous(array, axis):
    widths = [(0, 0)] * array.ndim
    widths[axis] = (1, 0)
    return lax.slice_in_dim(jnp.pad(array, widths), 0, array.shape[axis], axis=axis)


def following(array, axis):
    widths = [(0, 0)] * array.ndim
    widths[axis] = (0, 1)
    return lax.slice_in_dim(jnp.pad(array, widths), 1, array.shape[axis] + 1, axis=axis)


def place(before, after, axis):
    empty = jnp.zeros_like(before)
    return jnp.stack([before, empty, empty, after], axis=axis)


def neighbours(field):
    lattice = field.reshape(field.shape[:4] + (4, 4, 4) + field.shape[-1:])
    high_x = lattice[:, :, :, :, 3]
    low_x = lattice[:, :, :, :, 0]
    from_west = passed_along(high_x[:, -1], "sx", 1)
    from_east = passed_along(low_x[:, 0], "sx", -1)
    before_x = jnp.concatenate([from_west[:, None], high_x[:, :-1]], axis=1)
    after_x = jnp.concatenate([low_x[:, 1:], from_east[:, None]], axis=1)
    high_y = lattice[:, :, :, :, :, 3]
    low_y = lattice[:, :, :, :, :, 0]
    from_south = passed_along(high_y[:, :, -1], "sy", 1)
    from_north = passed_along(low_y[:, :, 0], "sy", -1)
    before_y = jnp.concatenate([from_south[:, :, None], high_y[:, :, :-1]], axis=2)
    after_y = jnp.concatenate([low_y[:, :, 1:], from_north[:, :, None]], axis=2)
    along_x = place(before_x, after_x, 4)
    along_y = place(before_y, after_y, 5)
    along_z = place(previous(lattice[..., 3, :], 6), following(lattice[..., 0, :], 6), 6)
    return (along_x + along_y + along_z).reshape(field.shape)


def apply_operator(field, coeff, flux_jacobian, laplace, grads, coupled):
    volume = jnp.einsum("mn,bxyfnz->bxyfmz", laplace, field, precision=HIGHEST)
    slopes = jnp.einsum("dmn,bxyfnz->dbxyfmz", grads, field, precision=HIGHEST)
    transport = jnp.einsum("dgf,dbxyfmz->bxygmz", flux_jacobian, slopes, precision=HIGHEST)
    return coeff * (volume - BETA * coupled) + transport


def precondition(residue, coeff, basis, spectrum, step):
    inverse = 1.0 / (1.0 + step * coeff * spectrum[:, None])
    modes = jnp.einsum("kn,bxyfnz->bxyfkz", basis, residue, precision=HIGHEST)
    return jnp.einsum("kn,bxyfkz->bxyfnz", basis, modes * inverse, precision=HIGHEST)


def block_jacobi(target, begin, force, step, turns, operate, solve):
    field = begin
    image = -force
    for turn in range(turns):
        if turn > 0:
            image = operate(field)
        field = field + solve(target - field - step * image, step)
    return field


def local_exchanging(initial, viscosity, flux_jacobian):
    laplace, grads, basis, spectrum = node_tables()
    coeff = viscosity[None, :, :, None, None, :]
    first_slice = lax.axis_index("tm") == 0

    def operate(field):
        return apply_operator(field, coeff, flux_jacobian, laplace, grads, neighbours(field))

    def solve(residue, step):
        return precondition(residue, coeff, basis, spectrum, step)

    start = initial[None]
    force_zero = -operate(start)
    values = [start, start, start]
    forces = [force_zero, force_zero, force_zero]
    for sweep in range(ITERS):
        old = list(forces)
        for node in range(2):
            weight = WEIGHTS[node]
            integral = STEP * (weight[0] * old[0] + weight[1] * old[1] + weight[2] * old[2])
            target = values[node] - HALF_STEP * old[node + 1] + integral
            values[node + 1] = block_jacobi(
                target, values[node + 1], old[node + 1], HALF_STEP, JF, operate, solve
            )
            forces[node + 1] = -operate(values[node + 1])
        correction = STEP * (TWO_THIRDS * forces[1] - ONE_THIRD * forces[0] - ONE_THIRD * forces[2])
        offset = -STEP * forces[2] + HALF_STEP * (forces[0] + forces[2]) + correction
        end_value = values[2]
        end_force = forces[2]

        def chain_turn(turn, carry):
            coarse_start, coarse_end = carry
            coarse_end = block_jacobi(
                coarse_start + offset, end_value, end_force, STEP, JC, operate, solve
            )
            passed = passed_along(coarse_end, "tm", 1)
            return (jnp.where(first_slice, start, passed), coarse_end)

        coarse_start, coarse_end = lax.fori_loop(0, lax.axis_size("tm"), chain_turn, (start, start))
        if sweep + 1 < ITERS:
            both = -operate(jnp.concatenate([coarse_start, coarse_end], axis=0))
            force_start = both[:1]
            force_end = both[1:]
            delta_start = force_start - forces[0]
            delta_end = force_end - forces[2]
            forces = [
                forces[0] + delta_start,
                forces[1] + 0.5 * (delta_start + delta_end),
                forces[2] + delta_end,
            ]
        move_start = coarse_start - values[0]
        move_end = coarse_end - values[2]
        values = [
            values[0] + move_start,
            values[1] + 0.5 * (move_start + move_end),
            values[2] + move_end,
        ]
    return jnp.stack(values, axis=1)


FIELDS = 5
ROWS = 320
SIZE = 2560
FACE = np.array([0.5] + [math.sqrt(0.5) * math.cos(math.pi * k / 8.0) for k in (1, 2, 3)])
PICK_1 = 4.0 * FACE[1] ** 2
PICK_3 = 4.0 * FACE[3] ** 2
MODES = [
    (a, b, c)
    for parity in (0, 1)
    for a in range(4)
    for b in range(4)
    for c in range(4)
    if (a + b + c) % 2 == parity
]
PLACE = {mode: (i // 32) * 160 + i % 32 for i, mode in enumerate(MODES)}
LEVELS = sorted({tuple(sorted(mode)) for mode in MODES})


def level(a, b, c):
    return LEVELS.index(tuple(sorted((a, b, c))))


def eigen(levels):
    line = [2.0 - 2.0 * math.cos(math.pi * k / 4.0) for k in range(4)]
    return sum(line[k] for k in levels) + SIGMA


def modal_tables():
    j = np.arange(4)
    cosine = np.cos(math.pi * j[:, None] * (2.0 * j[None, :] + 1.0) / 8.0)
    cosine *= np.where(j == 0, 0.5, math.sqrt(0.5))[:, None]
    basis = np.kron(np.kron(cosine, cosine), cosine)
    scale = np.kron(np.kron(FACE, FACE), FACE)
    order = [16 * a + 4 * b + c for a, b, c in MODES]
    into = (basis / scale[:, None])[order]
    back = (basis * scale[:, None])[order].T
    upper = np.eye(4, k=1)
    slope = 0.5 * upper - 0.5 * upper.T
    one = np.eye(4)
    grads = [
        np.kron(np.kron(slope, one), one),
        np.kron(np.kron(one, slope), one),
        np.kron(np.kron(one, one), slope),
    ]
    modal = np.stack([into @ grad @ back for grad in grads])
    blocks = np.stack([modal[:, 32:, :32], modal[:, :32, 32:]])
    return into, back, HALF_STEP * blocks


def three_pass(matrix):
    high = matrix.astype(jnp.bfloat16)
    low = (matrix - high.astype(np.float64)).astype(jnp.bfloat16)
    return jnp.asarray(np.concatenate([high, low, high], axis=1))


def split_rows(x):
    high = x.astype(jnp.bfloat16)
    low = (x - high.astype(jnp.float32)).astype(jnp.bfloat16)
    return jnp.concatenate([high, high, low], axis=0)


def steps(slices):
    start, temps = 0, 6 * slices + 2
    value = 4 * slices + 2
    work, first, mid, quad, base, zed, c0, hga = range(temps, temps + 8)
    plan = [(0, start, 0), (1, work, 0), (2, work, 0), (3, work, 0), (4, work, 0), (5, work, 0)]
    plan += [(6, mid, 0)]
    for t in range(slices):
        plan += [(7, work, t), (8, t + 1, t)]
    for kind in (9, 10, 9, 11):
        plan += [(kind, value + t, t) for t in range(slices)]
    plan += [(12, value + t, t) for t in reversed(range(slices))]
    plan += [(13, work, t) for t in range(slices)]
    return plan


def whole_grid_kernel(slices, plan, where, *refs):
    gathered, refs = refs[:8], refs[8:]
    matrix, into, back, out, st, tr, g, m, dh, dd, el, cc = refs
    f32 = jnp.float32
    slot_g = slices + 1
    slot_t = 2 * slices + 2
    slot_p = 3 * slices + 2
    slot_v = 4 * slices + 2
    slot_u = 5 * slices + 2
    work, first, mid, quad, base, zed, c0, hga = range(6 * slices + 2, 6 * slices + 10)

    for k in range(8):
        cc[pl.ds(where[2 + k], 1), :] = gathered[k][320:321, :]
    visc = cc[...]
    for i, levels in enumerate(LEVELS):
        lam = (HALF_STEP * eigen(levels)) * visc
        el[8 * i : 8 * i + 8, :] = lam
        dh[8 * i : 8 * i + 8, :] = 1.0 / (1.0 + lam)
        dd[8 * i : 8 * i + 8, :] = 1.0 / (1.0 + 2.0 * lam)
    for p in range(2):
        whole = matrix[p]
        high = whole.astype(jnp.bfloat16).astype(f32)
        lane = lax.broadcasted_iota(jnp.int32, whole.shape, 1)
        middle = (lane >= 160) & (lane < 320)
        m[p] = jnp.where(middle, whole - high, high).astype(jnp.bfloat16)
    for k in range(0, 8, 2):
        for f in range(FIELDS):
            x = jnp.concatenate([gathered[k + i][64 * f : 64 * f + 64, :] for i in (0, 1)], axis=1)
            r = jnp.dot(into[...], split_rows(x), preferred_element_type=f32)
            for i in (0, 1):
                for p in (0, 1):
                    at = p * 1280 + f * 256 + where[2 + k + i]
                    st[pl.ds(at, 32, 8), :] = r[32 * p : 32 * p + 32, 128 * i : 128 * i + 128]

    sub = lax.broadcasted_iota(jnp.int32, (8, 128), 0)
    lane = lax.broadcasted_iota(jnp.int32, (8, 128), 1)
    tau = jnp.where(sub >= 4, 1.0, -1.0).astype(f32)
    y_first, y_last = sub % 4 == 0, sub % 4 == 3
    z_first, z_last = lane == 0, lane == 127
    scaled = (HALF_STEP * BETA * 0.25) * visc

    def transport(src):
        at = src * SIZE

        def pair(jp, carry):
            for p in range(2):
                begin = at + p * 1280 + 2 * jp
                x = jnp.concatenate([st[pl.ds(begin + i, 160, 8), :] for i in (0, 1)], axis=1)
                r = jnp.dot(m[p], split_rows(x), preferred_element_type=f32)
                for i in (0, 1):
                    tr[pl.ds((1 - p) * 1280 + 2 * jp + i, 160, 8), :] = r[:, 128 * i : 128 * i + 128]
            return carry

        lax.fori_loop(0, 4, pair, 0)

    def faces(src):
        def field(f, carry):
            at = pl.multiple_of(src * SIZE + f * 256, 256)
            gat = pl.multiple_of(f * 128, 128)

            def ld(a, b, c):
                return st[pl.ds(at + 8 * PLACE[a, b, c], 8), :]

            for p in range(4):
                for q in range(4):
                    i = 8 * (4 * p + q)
                    even = ld(0, p, q) + ld(2, p, q)
                    odd = PICK_1 * ld(1, p, q) + PICK_3 * ld(3, p, q)
                    met = pltpu.roll(even + tau * odd, 4, 0)
                    g[pl.ds(gat + i, 8), :] = met
                    g[pl.ds(gat + 640 + i, 8), :] = tau * met
                    even = ld(p, 0, q) + ld(p, 2, q)
                    odd = PICK_1 * ld(p, 1, q) + PICK_3 * ld(p, 3, q)
                    low = jnp.where(y_first, 0.0, pltpu.roll(even - odd, 1, 0))
                    high = jnp.where(y_last, 0.0, pltpu.roll(even + odd, 7, 0))
                    g[pl.ds(gat + 1280 + i, 8), :] = low + high
                    g[pl.ds(gat + 1920 + i, 8), :] = low - high
                    even = ld(p, q, 0) + ld(p, q, 2)
                    odd = PICK_1 * ld(p, q, 1) + PICK_3 * ld(p, q, 3)
                    low = jnp.where(z_first, 0.0, pltpu.roll(even - odd, 1, 1))
                    high = jnp.where(z_last, 0.0, pltpu.roll(even + odd, 127, 1))
                    g[pl.ds(gat + 2560 + i, 8), :] = low + high
                    g[pl.ds(gat + 3200 + i, 8), :] = low - high
            return carry

        lax.fori_loop(0, FIELDS, field, 0)

    def finish(store):
        def field(f, carry):
            at = pl.multiple_of(f * 256, 256)
            gat = pl.multiple_of(f * 128, 128)
            for pa in range(2):
                for pb in range(2):
                    gx = {
                        (b, c): g[pl.ds(gat + 640 * pa + 8 * (4 * b + c), 8), :]
                        for b in (pb, pb + 2)
                        for c in range(4)
                    }
                    gy = {
                        (a, c): g[pl.ds(gat + 1280 + 640 * pb + 8 * (4 * a + c), 8), :]
                        for a in (pa, pa + 2)
                        for c in range(4)
                    }
                    for a in (pa, pa + 2):
                        for b in (pb, pb + 2):
                            gz = [
                                g[pl.ds(gat + 2560 + 640 * pc + 8 * (4 * a + b), 8), :]
                                for pc in range(2)
                            ]
                            for c in range(4):
                                row = at + 8 * PLACE[a, b, c]
                                n = gx[b, c] + gy[a, c] + gz[c % 2]
                                image = tr[pl.ds(row, 8), :] - scaled * n
                                store(row, level(a, b, c), image)
            return carry

        lax.fori_loop(0, FIELDS, field, 0)

    def ld(slot, row):
        return st[pl.ds(pl.multiple_of(slot * SIZE, SIZE) + row, 8), :]

    def put(slot, row, x):
        st[pl.ds(pl.multiple_of(slot * SIZE, SIZE) + row, 8), :] = x

    def tab(ref, i):
        return ref[8 * i : 8 * i + 8, :]

    def kind_0(t):
        def store(row, i, image):
            put(slot_g, row, image)
            put(work, row, tab(dh, i) * (ld(0, row) - image))

        finish(store)

    def kind_1(t):
        def store(row, i, image):
            put(work, row, tab(dh, i) * (ld(0, row) - image))

        finish(store)

    def kind_2(t):
        def store(row, i, image):
            u = tab(dh, i) * (ld(0, row) - image)
            put(first, row, u)
            put(work, row, tab(dh, i) * (u - ld(slot_g, row)))

        finish(store)

    def kind_3(t):
        def store(row, i, image):
            put(work, row, tab(dh, i) * (ld(first, row) - image))

        finish(store)

    def kind_4(t):
        def store(row, i, image):
            u1 = ld(first, row)
            u2 = tab(dh, i) * (u1 - image)
            start = ld(0, row)
            put(mid, row, u1 - 0.5 * (start + u2))
            put(work, row, (4.0 / 3.0) * u1 + (1.0 / 3.0) * u2)
            q = (5.0 / 6.0) * u2 - (2.0 / 3.0) * u1
            put(quad, row, q)
            lam = tab(el, i)
            put(base, row, lam * (2.0 * q - (1.0 / 3.0) * start) - (1.0 / 3.0) * ld(slot_g, row))

        finish(store)

    def kind_5(t):
        def store(row, i, image):
            z = ld(base, row) - image
            put(zed, row, z)
            put(work, row, 2.0 * (tab(dd, i) * (ld(0, row) + z) - ld(quad, row)))

        finish(store)

    def kind_6(t):
        def store(row, i, image):
            put(hga, row, image)
            put(c0, row, (1.0 / 3.0) * (tab(el, i) * ld(mid, row) + image))

        finish(store)

    def kind_7(t):
        def store(row, i, image):
            s = tab(dd, i) * (ld(t, row) + ld(base, row) - image)
            put(t + 1, row, s)
            put(work, row, 2.0 * (tab(dd, i) * (s + ld(zed, row)) - ld(quad, row)))

        finish(store)

    def kind_8(t):
        def store(row, i, image):
            put(slot_g + t + 1, row, image)
            s = ld(t, row)
            old = ld(slot_g + t, row)
            phi = 0.25 * (tab(el, i) * (ld(t + 1, row) - s) + image - old)
            c = ld(c0, row)
            target = s + phi + c
            put(slot_t + t, row, target)
            put(slot_p + t, row, phi - 2.0 * c)
            put(slot_v + t, row, tab(dh, i) * (target - ld(hga, row) - 0.5 * (old + image)))

        finish(store)

    def kind_9(t):
        def store(row, i, image):
            put(slot_v + t, row, tab(dh, i) * (ld(slot_t + t, row) - image))

        finish(store)

    def kind_10(t):
        def store(row, i, image):
            u = tab(dh, i) * (ld(slot_t + t, row) - image)
            put(slot_u + t, row, u)
            target = u + ld(slot_p + t, row)
            put(slot_t + t, row, target)
            put(slot_v + t, row, tab(dh, i) * (target - ld(slot_g + t + 1, row)))

        finish(store)

    def kind_11(t):
        def store(row, i, image):
            u1 = ld(slot_u + t, row)
            u2 = tab(dh, i) * (ld(slot_t + t, row) - image)
            s = ld(t, row)
            q = (5.0 / 6.0) * u2 - (2.0 / 3.0) * u1
            put(slot_p + t, row, q)
            put(slot_v + t, row, (4.0 / 3.0) * u1 + (1.0 / 3.0) * u2)
            put(slot_u + t, row, u1 - 0.5 * (s + u2))
            old = ld(slot_g + t, row)
            put(slot_t + t, row, tab(el, i) * (2.0 * q - (1.0 / 3.0) * s) - (1.0 / 3.0) * old)

        finish(store)

    def kind_12(t):
        def store(row, i, image):
            z = ld(slot_t + t, row) - image
            put(slot_v + t, row, z)
            put(work, row, 2.0 * (tab(dd, i) * (ld(0, row) + z) - ld(slot_p + t, row)))

        finish(store)

    def kind_13(t):
        later = jnp.minimum(t + 1, slices - 1)

        def store(row, i, image):
            s = tab(dd, i) * (ld(t, row) + ld(slot_t + t, row) - image)
            put(t + 1, row, s)
            z = ld(slot_v + later, row)
            put(work, row, 2.0 * (tab(dd, i) * (s + z) - ld(slot_p + later, row)))

        finish(store)

    kinds = [kind_0, kind_1, kind_2, kind_3, kind_4, kind_5, kind_6, kind_7, kind_8, kind_9]
    kinds += [kind_10, kind_11, kind_12, kind_13]

    def step(n, carry):
        transport(plan[3 * n + 1])
        faces(plan[3 * n + 1])
        lax.switch(plan[3 * n], kinds, plan[3 * n + 2])
        return carry

    lax.fori_loop(0, len(steps(slices)), step, 0)

    mine, column = where[0], where[1]
    for f in range(FIELDS):

        def own(slot):
            at = slot * SIZE + f * 256 + column
            return jnp.concatenate([st[pl.ds(at + 1280 * p, 32, 8), :] for p in (0, 1)], axis=0)

        begin, end = own(mine), own(mine + 1)
        middle = own(slot_u + mine) + 0.5 * (begin + end)
        x = jnp.concatenate([begin, middle, end], axis=1)
        r = jnp.dot(back[...], split_rows(x), preferred_element_type=f32)
        for i in range(3):
            out[i, 64 * f : 64 * f + 64, :] = r[:, 128 * i : 128 * i + 128]


def local_whole_grid(slices):
    def local(initial, viscosity, flux_jacobian):
        block = jnp.concatenate(
            [initial.reshape(ROWS, 128), jnp.broadcast_to(viscosity.reshape(1, 128), (8, 128))], axis=0
        )
        near = [block]
        for k in range(1, 4):
            near.append(lax.ppermute(block, "sy", [(i, i ^ k) for i in range(4)]))
        gathered = near + [lax.ppermute(b, "sx", [(0, 1), (1, 0)]) for b in near]

        x, y = lax.axis_index("sx"), lax.axis_index("sy")
        columns = [(x ^ (k // 4)) * 4 + (y ^ (k % 4)) for k in range(8)]
        where = jnp.stack([lax.axis_index("tm"), x * 4 + y] + columns).astype(jnp.int32)
        plan = jnp.asarray(np.array(steps(slices), np.int32).reshape(-1))

        into, back, blocks = modal_tables()
        tables = jnp.asarray(blocks, jnp.float32)
        matrix = sum(
            flux_jacobian[d][None, :, None, :, None] * tables[:, d, None, :, None, :] for d in range(3)
        ).reshape(2, 160, 160)
        matrix = jnp.concatenate([matrix, matrix, matrix], axis=2)

        smem = pl.BlockSpec(memory_space=pltpu.SMEM)
        vmem = pl.BlockSpec(memory_space=pltpu.VMEM)

        def scratch(rows):
            return pltpu.VMEM((rows, 128), jnp.float32)

        out = pl.pallas_call(
            lambda plan, where, *refs: whole_grid_kernel(slices, plan, where, *refs),
            out_shape=jax.ShapeDtypeStruct((3, ROWS, 128), jnp.float32),
            in_specs=[smem, smem] + [vmem] * 11,
            out_specs=vmem,
            scratch_shapes=[
                scratch((6 * slices + 10) * SIZE),
                scratch(SIZE),
                scratch(3840),
                pltpu.VMEM((2, 160, 480), jnp.bfloat16),
                scratch(8 * len(LEVELS)),
                scratch(8 * len(LEVELS)),
                scratch(8 * len(LEVELS)),
                scratch(8),
            ],
            compiler_params=pltpu.CompilerParams(vmem_limit_bytes=58 << 20),
        )(plan, where, *gathered, matrix, three_pass(into), three_pass(back))
        return out.reshape(1, 3, 1, 1, FIELDS, 64, 128)

    return local


def solution(mesh):
    grid = (mesh.shape["sx"], mesh.shape["sy"])
    slices = mesh.shape["tm"]
    local = local_whole_grid(slices) if grid == (2, 4) and slices <= 4 else local_exchanging
    return jax.shard_map(
        local,
        mesh=mesh,
        in_specs=(P("sx", "sy", None, None, None), P("sx", "sy", None), P()),
        out_specs=P("tm", None, "sx", "sy", None, None, None),
        check_vma=False,
    )
```

profile of v0, /device:TPU:0, one launch (start us, length us, event | category | flops | bytes accessed | tf_op | source)
XLA Modules:
  0.0 150.1 jit_solution(8957122655239944058)
XLA Ops:
  0.0 0.7 broadcast_in_dim.8
  0.7 0.9 pad_maximum_fusion.1.refs_0_
  1.6 0.0 copy-start
  1.6 3.0 %collective-permute-start = (f32[328,128]{1,0:T(8,128)S(1)}, f32[328,128]{1,0:T(8,128)S(1)}, u32[]{:S(2)}, u32[]{:S(2)}) collective-permute-start(f32[328,128]{1,0:T(8,128)S(1)} %pad_maximum_fusion.1.refs_0_), channel_id=1, source_target_pairs={{0,1},{1,0},{2,3},{3,2},{4,5},{5,4},{6,7},{7,6},{8,9},{9,8},{10,11... | collective-permute-start | bytes 503816 | tf_op jit(solution)/shard_map/ppermute | solution.py:553
  4.6 1.5 %collective-permute-start.1 = (f32[328,128]{1,0:T(8,128)S(1)}, f32[328,128]{1,0:T(8,128)S(1)}, u32[]{:S(2)}, u32[]{:S(2)}) collective-permute-start(f32[328,128]{1,0:T(8,128)S(1)} %pad_maximum_fusion.1.refs_0_), channel_id=1, source_target_pairs={{0,2},{1,3},{2,0},{3,1},{4,6},{5,7},{6,4},{7,5},{8,10},{9,11},{10,... | collective-permute-start | bytes 503816 | tf_op jit(solution)/shard_map/ppermute | solution.py:553
  6.1 0.0 collective-permute-start.2
  6.1 0.0 collective-permute-start.3
  6.1 0.8 fusion
  7.0 0.1 mul.104
  7.1 0.1 mul.105
  7.2 0.1 mul.96
  7.3 0.0 copy-start.8
  7.4 0.1 mul.97
  7.5 0.0 copy-done
  7.5 0.1 mul.88
  7.6 0.1 mul.89
  7.8 0.3 copy-done.8
  8.1 0.0 copy-start.9
  8.1 0.1 mul.100
  8.2 0.3 mul.101
  8.5 0.4 copy-done.9
  8.9 0.0 copy-start.7
  8.9 0.1 mul.108
  9.0 0.3 mul.109
  9.2 0.4 copy-done.7
  9.6 0.1 mul.92
  9.7 0.3 mul.93
  10.0 0.0 collective-permute-done.refs_1_
  10.0 0.0 copy-start.1
  10.0 0.6 collective-permute-start.4
  10.6 3.4 %collective-permute-done.1.refs_2_ = f32[328,128]{1,0:T(8,128)S(1)} collective-permute-done((f32[328,128]{1,0:T(8,128)S(1)}, f32[328,128]{1,0:T(8,128)S(1)}, u32[]{:S(2)}, u32[]{:S(2)}) %collective-permute-start.1) | collective-permute-done | bytes 167968 | tf_op jit(solution)/shard_map/ppermute | solution.py:553
  13.9 0.0 copy-start.2
  13.9 0.0 collective-permute-start.5
  14.0 0.0 collective-permute-done.2.refs_3_
  14.0 0.0 copy-start.3
  14.0 0.5 collective-permute-start.6
  14.5 0.1 multiply_add_fusion
  14.6 0.6 stack.40.where
  15.2 1.1 pad_maximum_fusion.refs_8_
  16.3 0.0 copy-done.1
  16.3 0.0 copy-done.2
  16.3 0.0 copy-done.3
  16.3 0.0 collective-permute-done.3.refs_4_
  16.3 0.0 collective-permute-done.4.refs_5_
  16.3 0.0 copy-start.4
  16.3 0.0 collective-permute-done.5.refs_6_
  16.4 0.0 copy-start.5
  16.4 0.0 collective-permute-done.6.refs_7_
  16.4 0.6 copy-done.4
  17.0 0.1 copy-done.5
  17.1 0.0 copy-start.6
  17.1 0.7 copy-done.6
  17.7 132.4 %shard_map.73 = f32[3,320,128]{2,1,0:T(8,128)} custom-call(s32[117]{0:T(128)} %constant.28.clone.plan, s32[10]{0:T(128)} %stack.40.where, f32[328,128]{1,0:T(8,128)} %copy-done, f32[328,128]{1,0:T(8,128)} %copy-done.1, f32[328,128]{1,0:T(8,128)} %copy-done.2, f32[328,128]{1,0:T(8,128)} %copy-done.3, f32[328,128]{1,0:T(8,128)} %collective-permute-done.3.refs_4_, ...), custom_call_target="tpu_custom_call" | custom-call | tf_op jit(solution)/shard_map/pallas_call | solution.py:574
  (2 shorter events, 0.0 us)
Async XLA Ops:
  1.6 5.9 %copy-start = (f32[328,128]{1,0:T(8,128)}, f32[328,128]{1,0:T(8,128)S(1)}, u32[]{:S(2)}) copy-start(f32[328,128]{1,0:T(8,128)S(1)} %pad_maximum_fusion.1.refs_0_) | copy-start | bytes 503812
  1.6 8.4 %collective-permute-start = (f32[328,128]{1,0:T(8,128)S(1)}, f32[328,128]{1,0:T(8,128)S(1)}, u32[]{:S(2)}, u32[]{:S(2)}) collective-permute-start(f32[328,128]{1,0:T(8,128)S(1)} %pad_maximum_fusion.1.refs_0_), channel_id=1, source_target_pairs={{0,1},{1,0},{2,3},{3,2},{4,5},{5,4},{6,7},{7,6},{8,9},{9,8},{10,11... | collective-permute-start | bytes 503816 | tf_op jit(solution)/shard_map/ppermute | solution.py:553
  4.6 9.3 %collective-permute-start.1 = (f32[328,128]{1,0:T(8,128)S(1)}, f32[328,128]{1,0:T(8,128)S(1)}, u32[]{:S(2)}, u32[]{:S(2)}) collective-permute-start(f32[328,128]{1,0:T(8,128)S(1)} %pad_maximum_fusion.1.refs_0_), channel_id=1, source_target_pairs={{0,2},{1,3},{2,0},{3,1},{4,6},{5,7},{6,4},{7,5},{8,10},{9,11},{10,... | collective-permute-start | bytes 503816 | tf_op jit(solution)/shard_map/ppermute | solution.py:553
  6.1 7.8 %collective-permute-start.2 = (f32[328,128]{1,0:T(8,128)S(1)}, f32[328,128]{1,0:T(8,128)S(1)}, u32[]{:S(2)}, u32[]{:S(2)}) collective-permute-start(f32[328,128]{1,0:T(8,128)S(1)} %pad_maximum_fusion.1.refs_0_), channel_id=1, source_target_pairs={{0,3},{1,2},{2,1},{3,0},{4,7},{5,6},{6,5},{7,4},{8,11},{9,10},{10,... | collective-permute-start | bytes 503816 | tf_op jit(solution)/shard_map/ppermute | solution.py:553
  6.1 10.2 %collective-permute-start.3 = (f32[328,128]{1,0:T(8,128)S(1)}, f32[328,128]{1,0:T(8,128)}, u32[]{:S(2)}, u32[]{:S(2)}) collective-permute-start(f32[328,128]{1,0:T(8,128)S(1)} %pad_maximum_fusion.1.refs_0_), channel_id=1, source_target_pairs={{0,4},{4,0},{1,5},{5,1},{2,6},{6,2},{3,7},{7,3},{8,12},{12,8},{9,1... | collective-permute-start | bytes 503816 | tf_op jit(solution)/shard_map/ppermute | solution.py:554
  7.3 0.8 copy-start.8
  8.1 0.8 copy-start.9
  8.9 0.8 copy-start.7
  10.0 6.3 %copy-start.1 = (f32[328,128]{1,0:T(8,128)}, f32[328,128]{1,0:T(8,128)S(1)}, u32[]{:S(2)}) copy-start(f32[328,128]{1,0:T(8,128)S(1)} %collective-permute-done.refs_1_) | copy-start | bytes 503812
  10.0 6.3 %collective-permute-start.4 = (f32[328,128]{1,0:T(8,128)S(1)}, f32[328,128]{1,0:T(8,128)S(1)}, u32[]{:S(2)}, u32[]{:S(2)}) collective-permute-start(f32[328,128]{1,0:T(8,128)S(1)} %collective-permute-done.refs_1_), channel_id=1, source_target_pairs={{0,4},{4,0},{1,5},{5,1},{2,6},{6,2},{3,7},{7,3},{8,12},{12,8},{9,1... | collective-permute-start | bytes 503816 | tf_op jit(solution)/shard_map/ppermute | solution.py:554
  13.9 2.4 %copy-start.2 = (f32[328,128]{1,0:T(8,128)}, f32[328,128]{1,0:T(8,128)S(1)}, u32[]{:S(2)}) copy-start(f32[328,128]{1,0:T(8,128)S(1)} %collective-permute-done.1.refs_2_) | copy-start | bytes 503812
  13.9 2.4 %collective-permute-start.5 = (f32[328,128]{1,0:T(8,128)S(1)}, f32[328,128]{1,0:T(8,128)S(1)}, u32[]{:S(2)}, u32[]{:S(2)}) collective-permute-start(f32[328,128]{1,0:T(8,128)S(1)} %collective-permute-done.1.refs_2_), channel_id=1, source_target_pairs={{0,4},{4,0},{1,5},{5,1},{2,6},{6,2},{3,7},{7,3},{8,12},{12,8},{9,1... | collective-permute-start | bytes 503816 | tf_op jit(solution)/shard_map/ppermute | solution.py:554
  14.0 2.4 %copy-start.3 = (f32[328,128]{1,0:T(8,128)}, f32[328,128]{1,0:T(8,128)S(1)}, u32[]{:S(2)}) copy-start(f32[328,128]{1,0:T(8,128)S(1)} %collective-permute-done.2.refs_3_) | copy-start | bytes 503812
  14.0 2.4 %collective-permute-start.6 = (f32[328,128]{1,0:T(8,128)S(1)}, f32[328,128]{1,0:T(8,128)S(1)}, u32[]{:S(2)}, u32[]{:S(2)}) collective-permute-start(f32[328,128]{1,0:T(8,128)S(1)} %collective-permute-done.2.refs_3_), channel_id=1, source_target_pairs={{0,4},{4,0},{1,5},{5,1},{2,6},{6,2},{3,7},{7,3},{8,12},{12,8},{9,1... | collective-permute-start | bytes 503816 | tf_op jit(solution)/shard_map/ppermute | solution.py:554
  16.3 0.7 copy-start.4
  16.4 0.7 copy-start.5
  17.1 0.7 copy-start.6
where the time goes:
time: 150 us
  Pallas kernels  132 us (88%)
  local copies, waits for them, and re-layouts  6.39 us (4%)
  starting transfers between devices  5.62 us (4%)
  waiting for transfers between devices  3.38 us (2%)
  other arithmetic  2.15 us (1%)
    pallas_call x1, Pallas kernels, local(): pl.pallas_call(lambda plan, where, *refs: whole_grid_kernel(slices, plan,...  132 us
    ppermute x3, starting transfers between devices, local(): near.append(lax.ppermute(block, 'sy', [(i, i ^ k) for i in range(4)]))  4.54 us
    ppermute x3, waiting for transfers between devices, local(): near.append(lax.ppermute(block, 'sy', [(i, i ^ k) for i in range(4)]))  3.37 us
  transfers between devices with their start and end apart: 7, of which 1 were waited for; matrix products, arithmetic and copies ran while one was open for 3% of the time, Pallas kernels for 0%

commit v1 on v0

--- a/solution.py
+++ b/solution.py
@@ -249,30 +249,24 @@
 
 
 def steps(slices):
-    start, temps = 0, 6 * slices + 2
-    value = 4 * slices + 2
-    work, first, mid, quad, base, zed, c0, hga = range(temps, temps + 8)
-    plan = [(0, start, 0), (1, work, 0), (2, work, 0), (3, work, 0), (4, work, 0), (5, work, 0)]
+    work, mid, copy = slices, slices + 1, slices + 2
+    plan = [(0, work, 0), (1, work, 0), (2, work, 0), (3, work, 0), (4, work, 0), (5, work, 0)]
     plan += [(6, mid, 0)]
     for t in range(slices):
-        plan += [(7, work, t), (8, t + 1, t)]
+        plan += [(7, work, t), (8, copy, t)]
     for kind in (9, 10, 9, 11):
-        plan += [(kind, value + t, t) for t in range(slices)]
-    plan += [(12, value + t, t) for t in reversed(range(slices))]
+        plan += [(kind, t, t) for t in range(slices)]
+    plan += [(12, t, t) for t in reversed(range(slices))]
     plan += [(13, work, t) for t in range(slices)]
     return plan
 
 
 def whole_grid_kernel(slices, plan, where, *refs):
     gathered, refs = refs[:8], refs[8:]
-    matrix, into, back, out, st, tr, g, m, dh, dd, el, cc = refs
+    matrix, into, back, out, *refs = refs
+    ss, gg, tt, pp, vv, uu, first, quad, base, zed, c0, hga, tr, g, m, dh, dd, el, cc = refs
     f32 = jnp.float32
-    slot_g = slices + 1
-    slot_t = 2 * slices + 2
-    slot_p = 3 * slices + 2
-    slot_v = 4 * slices + 2
-    slot_u = 5 * slices + 2
-    work, first, mid, quad, base, zed, c0, hga = range(6 * slices + 2, 6 * slices + 10)
+    work, mid, copy = slices * SIZE, (slices + 1) * SIZE, (slices + 2) * SIZE
 
     for k in range(8):
         cc[pl.ds(where[2 + k], 1), :] = gathered[k][320:321, :]
@@ -295,7 +289,9 @@
             for i in (0, 1):
                 for p in (0, 1):
                     at = p * 1280 + f * 256 + where[2 + k + i]
-                    st[pl.ds(at, 32, 8), :] = r[32 * p : 32 * p + 32, 128 * i : 128 * i + 128]
+                    part = r[32 * p : 32 * p + 32, 128 * i : 128 * i + 128]
+                    ss[pl.ds(at, 32, 8), :] = part
+                    vv[pl.ds(work + at, 32, 8), :] = part
 
     sub = lax.broadcasted_iota(jnp.int32, (8, 128), 0)
     lane = lax.broadcasted_iota(jnp.int32, (8, 128), 1)
@@ -304,51 +300,42 @@
     z_first, z_last = lane == 0, lane == 127
     scaled = (HALF_STEP * BETA * 0.25) * visc
 
-    def transport(src):
-        at = src * SIZE
-
-        def pair(jp, carry):
+    def transport(at):
+        for jp in range(4):
             for p in range(2):
-                begin = at + p * 1280 + 2 * jp
-                x = jnp.concatenate([st[pl.ds(begin + i, 160, 8), :] for i in (0, 1)], axis=1)
+                begin = at + (p * 1280 + 2 * jp)
+                x = jnp.concatenate([vv[pl.ds(begin + i, 160, 8), :] for i in (0, 1)], axis=1)
                 r = jnp.dot(m[p], split_rows(x), preferred_element_type=f32)
                 for i in (0, 1):
                     tr[pl.ds((1 - p) * 1280 + 2 * jp + i, 160, 8), :] = r[:, 128 * i : 128 * i + 128]
-            return carry
-
-        lax.fori_loop(0, 4, pair, 0)
-
-    def faces(src):
-        def field(f, carry):
-            at = pl.multiple_of(src * SIZE + f * 256, 256)
-            gat = pl.multiple_of(f * 128, 128)
-
-            def ld(a, b, c):
-                return st[pl.ds(at + 8 * PLACE[a, b, c], 8), :]
-
+            yield
+
+    def faces(at_x, at_y, at_z):
+        def ld(at, a, b, c):
+            return vv[pl.ds(at + (256 * f + 8 * PLACE[a, b, c]), 8), :]
+
+        for f in range(FIELDS):
             for p in range(4):
                 for q in range(4):
-                    i = 8 * (4 * p + q)
-                    even = ld(0, p, q) + ld(2, p, q)
-                    odd = PICK_1 * ld(1, p, q) + PICK_3 * ld(3, p, q)
+                    i = 8 * (16 * f + 4 * p + q)
+                    even = ld(at_x, 0, p, q) + ld(at_x, 2, p, q)
+                    odd = PICK_1 * ld(at_x, 1, p, q) + PICK_3 * ld(at_x, 3, p, q)
                     met = pltpu.roll(even + tau * odd, 4, 0)
-                    g[pl.ds(gat + i, 8), :] = met
-                    g[pl.ds(gat + 640 + i, 8), :] = tau * met
-                    even = ld(p, 0, q) + ld(p, 2, q)
-                    odd = PICK_1 * ld(p, 1, q) + PICK_3 * ld(p, 3, q)
+                    g[i : i + 8, :] = met
+                    g[640 + i : 648 + i, :] = tau * met
+                    even = ld(at_y, p, 0, q) + ld(at_y, p, 2, q)
+                    odd = PICK_1 * ld(at_y, p, 1, q) + PICK_3 * ld(at_y, p, 3, q)
                     low = jnp.where(y_first, 0.0, pltpu.roll(even - odd, 1, 0))
                     high = jnp.where(y_last, 0.0, pltpu.roll(even + odd, 7, 0))
-                    g[pl.ds(gat + 1280 + i, 8), :] = low + high
-                    g[pl.ds(gat + 1920 + i, 8), :] = low - high
-                    even = ld(p, q, 0) + ld(p, q, 2)
-                    odd = PICK_1 * ld(p, q, 1) + PICK_3 * ld(p, q, 3)
+                    g[1280 + i : 1288 + i, :] = low + high
+                    g[1920 + i : 1928 + i, :] = low - high
+                    even = ld(at_z, p, q, 0) + ld(at_z, p, q, 2)
+                    odd = PICK_1 * ld(at_z, p, q, 1) + PICK_3 * ld(at_z, p, q, 3)
                     low = jnp.where(z_first, 0.0, pltpu.roll(even - odd, 1, 1))
                     high = jnp.where(z_last, 0.0, pltpu.roll(even + odd, 127, 1))
-                    g[pl.ds(gat + 2560 + i, 8), :] = low + high
-                    g[pl.ds(gat + 3200 + i, 8), :] = low - high
-            return carry
-
-        lax.fori_loop(0, FIELDS, field, 0)
+                    g[2560 + i : 2568 + i, :] = low + high
+                    g[3200 + i : 3208 + i, :] = low - high
+            yield
 
     def finish(store):
         def field(f, carry):
@@ -357,63 +344,63 @@
             for pa in range(2):
                 for pb in range(2):
                     gx = {
-                        (b, c): g[pl.ds(gat + 640 * pa + 8 * (4 * b + c), 8), :]
+                        (b, c): g[pl.ds(gat + (640 * pa + 8 * (4 * b + c)), 8), :]
                         for b in (pb, pb + 2)
                         for c in range(4)
                     }
                     gy = {
-                        (a, c): g[pl.ds(gat + 1280 + 640 * pb + 8 * (4 * a + c), 8), :]
+                        (a, c): g[pl.ds(gat + (1280 + 640 * pb + 8 * (4 * a + c)), 8), :]
                         for a in (pa, pa + 2)
                         for c in range(4)
                     }
                     for a in (pa, pa + 2):
                         for b in (pb, pb + 2):
                             gz = [
-                                g[pl.ds(gat + 2560 + 640 * pc + 8 * (4 * a + b), 8), :]
+                                g[pl.ds(gat + (2560 + 640 * pc + 8 * (4 * a + b)), 8), :]
                                 for pc in range(2)
                             ]
                             for c in range(4):
-                                row = at + 8 * PLACE[a, b, c]
+                                row = 8 * PLACE[a, b, c]
                                 n = gx[b, c] + gy[a, c] + gz[c % 2]
-                                image = tr[pl.ds(row, 8), :] - scaled * n
-                                store(row, level(a, b, c), image)
+                                image = tr[pl.ds(at + row, 8), :] - scaled * n
+                                store((at, row), level(a, b, c), image)
             return carry
 
         lax.fori_loop(0, FIELDS, field, 0)
 
-    def ld(slot, row):
-        return st[pl.ds(pl.multiple_of(slot * SIZE, SIZE) + row, 8), :]
-
-    def put(slot, row, x):
-        st[pl.ds(pl.multiple_of(slot * SIZE, SIZE) + row, 8), :] = x
+    def ld(ref, row, start=0, more=0):
+        return ref[pl.ds(pl.multiple_of(start + row[0], 256) + (more + row[1]), 8), :]
+
+    def put(ref, row, x, start=0, more=0):
+        ref[pl.ds(pl.multiple_of(start + row[0], 256) + (more + row[1]), 8), :] = x
 
     def tab(ref, i):
         return ref[8 * i : 8 * i + 8, :]
 
     def kind_0(t):
         def store(row, i, image):
-            put(slot_g, row, image)
-            put(work, row, tab(dh, i) * (ld(0, row) - image))
+            put(gg, row, image)
+            put(vv, row, tab(dh, i) * (ld(ss, row) - image), 0, work)
 
         finish(store)
 
     def kind_1(t):
         def store(row, i, image):
-            put(work, row, tab(dh, i) * (ld(0, row) - image))
+            put(vv, row, tab(dh, i) * (ld(ss, row) - image), 0, work)
 
         finish(store)
 
     def kind_2(t):
         def store(row, i, image):
-            u = tab(dh, i) * (ld(0, row) - image)
+            u = tab(dh, i) * (ld(ss, row) - image)
             put(first, row, u)
-            put(work, row, tab(dh, i) * (u - ld(slot_g, row)))
+            put(vv, row, tab(dh, i) * (u - ld(gg, row)), 0, work)
 
         finish(store)
 
     def kind_3(t):
         def store(row, i, image):
-            put(work, row, tab(dh, i) * (ld(first, row) - image))
+            put(vv, row, tab(dh, i) * (ld(first, row) - image), 0, work)
 
         finish(store)
 
@@ -421,13 +408,13 @@
         def store(row, i, image):
             u1 = ld(first, row)
             u2 = tab(dh, i) * (u1 - image)
-            start = ld(0, row)
-            put(mid, row, u1 - 0.5 * (start + u2))
-            put(work, row, (4.0 / 3.0) * u1 + (1.0 / 3.0) * u2)
+            start = ld(ss, row)
+            put(vv, row, u1 - 0.5 * (start + u2), 0, mid)
+            put(vv, row, (4.0 / 3.0) * u1 + (1.0 / 3.0) * u2, 0, work)
             q = (5.0 / 6.0) * u2 - (2.0 / 3.0) * u1
             put(quad, row, q)
             lam = tab(el, i)
-            put(base, row, lam * (2.0 * q - (1.0 / 3.0) * start) - (1.0 / 3.0) * ld(slot_g, row))
+            put(base, row, lam * (2.0 * q - (1.0 / 3.0) * start) - (1.0 / 3.0) * ld(gg, row))
 
         finish(store)
 
@@ -435,85 +422,99 @@
         def store(row, i, image):
             z = ld(base, row) - image
             put(zed, row, z)
-            put(work, row, 2.0 * (tab(dd, i) * (ld(0, row) + z) - ld(quad, row)))
+            put(vv, row, 2.0 * (tab(dd, i) * (ld(ss, row) + z) - ld(quad, row)), 0, work)
 
         finish(store)
 
     def kind_6(t):
         def store(row, i, image):
             put(hga, row, image)
-            put(c0, row, (1.0 / 3.0) * (tab(el, i) * ld(mid, row) + image))
+            put(c0, row, (1.0 / 3.0) * (tab(el, i) * ld(vv, row, 0, mid) + image))
 
         finish(store)
 
     def kind_7(t):
-        def store(row, i, image):
-            s = tab(dd, i) * (ld(t, row) + ld(base, row) - image)
-            put(t + 1, row, s)
-            put(work, row, 2.0 * (tab(dd, i) * (s + ld(zed, row)) - ld(quad, row)))
+        at = t * SIZE
+
+        def store(row, i, image):
+            s = tab(dd, i) * (ld(ss, row, at) + ld(base, row) - image)
+            put(ss, row, s, at, SIZE)
+            put(vv, row, s, 0, copy)
+            put(vv, row, 2.0 * (tab(dd, i) * (s + ld(zed, row)) - ld(quad, row)), 0, work)
 
         finish(store)
 
     def kind_8(t):
-        def store(row, i, image):
-            put(slot_g + t + 1, row, image)
-            s = ld(t, row)
-            old = ld(slot_g + t, row)
-            phi = 0.25 * (tab(el, i) * (ld(t + 1, row) - s) + image - old)
+        at = t * SIZE
+
+        def store(row, i, image):
+            put(gg, row, image, at, SIZE)
+            s = ld(ss, row, at)
+            old = ld(gg, row, at)
+            phi = 0.25 * (tab(el, i) * (ld(ss, row, at, SIZE) - s) + image - old)
             c = ld(c0, row)
             target = s + phi + c
-            put(slot_t + t, row, target)
-            put(slot_p + t, row, phi - 2.0 * c)
-            put(slot_v + t, row, tab(dh, i) * (target - ld(hga, row) - 0.5 * (old + image)))
+            put(tt, row, target, at)
+            put(pp, row, phi - 2.0 * c, at)
+            put(vv, row, tab(dh, i) * (target - ld(hga, row) - 0.5 * (old + image)), at)
 
         finish(store)
 
     def kind_9(t):
-        def store(row, i, image):
-            put(slot_v + t, row, tab(dh, i) * (ld(slot_t + t, row) - image))
+        at = t * SIZE
+
+        def store(row, i, image):
+            put(vv, row, tab(dh, i) * (ld(tt, row, at) - image), at)
 
         finish(store)
 
     def kind_10(t):
-        def store(row, i, image):
-            u = tab(dh, i) * (ld(slot_t + t, row) - image)
-            put(slot_u + t, row, u)
-            target = u + ld(slot_p + t, row)
-            put(slot_t + t, row, target)
-            put(slot_v + t, row, tab(dh, i) * (target - ld(slot_g + t + 1, row)))
+        at = t * SIZE
+
+        def store(row, i, image):
+            u = tab(dh, i) * (ld(tt, row, at) - image)
+            put(uu, row, u, at)
+            target = u + ld(pp, row, at)
+            put(tt, row, target, at)
+            put(vv, row, tab(dh, i) * (target - ld(gg, row, at, SIZE)), at)
 
         finish(store)
 
     def kind_11(t):
-        def store(row, i, image):
-            u1 = ld(slot_u + t, row)
-            u2 = tab(dh, i) * (ld(slot_t + t, row) - image)
-            s = ld(t, row)
+        at = t * SIZE
+
+        def store(row, i, image):
+            u1 = ld(uu, row, at)
+            u2 = tab(dh, i) * (ld(tt, row, at) - image)
+            s = ld(ss, row, at)
             q = (5.0 / 6.0) * u2 - (2.0 / 3.0) * u1
-            put(slot_p + t, row, q)
-            put(slot_v + t, row, (4.0 / 3.0) * u1 + (1.0 / 3.0) * u2)
-            put(slot_u + t, row, u1 - 0.5 * (s + u2))
-            old = ld(slot_g + t, row)
-            put(slot_t + t, row, tab(el, i) * (2.0 * q - (1.0 / 3.0) * s) - (1.0 / 3.0) * old)
+            put(pp, row, q, at)
+            put(vv, row, (4.0 / 3.0) * u1 + (1.0 / 3.0) * u2, at)
+            put(uu, row, u1 - 0.5 * (s + u2), at)
+            old = ld(gg, row, at)
+            put(tt, row, tab(el, i) * (2.0 * q - (1.0 / 3.0) * s) - (1.0 / 3.0) * old, at)
 
         finish(store)
 
     def kind_12(t):
-        def store(row, i, image):
-            z = ld(slot_t + t, row) - image
-            put(slot_v + t, row, z)
-            put(work, row, 2.0 * (tab(dd, i) * (ld(0, row) + z) - ld(slot_p + t, row)))
+        at = t * SIZE
+
+        def store(row, i, image):
+            z = ld(tt, row, at) - image
+            put(gg, row, z, at)
+            put(vv, row, 2.0 * (tab(dd, i) * (ld(ss, row) + z) - ld(pp, row, at)), 0, work)
 
         finish(store)
 
     def kind_13(t):
-        later = jnp.minimum(t + 1, slices - 1)
-
-        def store(row, i, image):
-            s = tab(dd, i) * (ld(t, row) + ld(slot_t + t, row) - image)
-            put(t + 1, row, s)
-            z = ld(slot_v + later, row)
-            put(work, row, 2.0 * (tab(dd, i) * (s + z) - ld(slot_p + later, row)))
+        at = t * SIZE
+        later = jnp.minimum(t + 1, slices - 1) * SIZE
+
+        def store(row, i, image):
+            s = tab(dd, i) * (ld(ss, row, at) + ld(tt, row, at) - image)
+            put(ss, row, s, at, SIZE)
+            z = ld(gg, row, later)
+            put(vv, row, 2.0 * (tab(dd, i) * (s + z) - ld(pp, row, later)), 0, work)
 
         finish(store)
 
@@ -521,9 +522,11 @@
     kinds += [kind_10, kind_11, kind_12, kind_13]
 
     def step(n, carry):
-        transport(plan[3 * n + 1])
-        faces(plan[3 * n + 1])
-        lax.switch(plan[3 * n], kinds, plan[3 * n + 2])
+        at = [pl.multiple_of(plan[5 * n + i], SIZE) for i in range(1, 4)]
+        one, other = transport(at[0]), faces(*at)
+        for _ in other:
+            next(one, None)
+        lax.switch(plan[5 * n], kinds, plan[5 * n + 4])
         return carry
 
     lax.fori_loop(0, len(steps(slices)), step, 0)
@@ -531,12 +534,12 @@
     mine, column = where[0], where[1]
     for f in range(FIELDS):
 
-        def own(slot):
+        def own(ref, slot):
             at = slot * SIZE + f * 256 + column
-            return jnp.concatenate([st[pl.ds(at + 1280 * p, 32, 8), :] for p in (0, 1)], axis=0)
-
-        begin, end = own(mine), own(mine + 1)
-        middle = own(slot_u + mine) + 0.5 * (begin + end)
+            return jnp.concatenate([ref[pl.ds(at + 1280 * p, 32, 8), :] for p in (0, 1)], axis=0)
+
+        begin, end = own(ss, mine), own(ss, mine + 1)
+        middle = own(uu, mine) + 0.5 * (begin + end)
         x = jnp.concatenate([begin, middle, end], axis=1)
         r = jnp.dot(back[...], split_rows(x), preferred_element_type=f32)
         for i in range(3):
@@ -556,7 +559,8 @@
         x, y = lax.axis_index("sx"), lax.axis_index("sy")
         columns = [(x ^ (k // 4)) * 4 + (y ^ (k % 4)) for k in range(8)]
         where = jnp.stack([lax.axis_index("tm"), x * 4 + y] + columns).astype(jnp.int32)
-        plan = jnp.asarray(np.array(steps(slices), np.int32).reshape(-1))
+        plan = [(kind, at * SIZE, at * SIZE, at * SIZE, t) for kind, at, t in steps(slices)]
+        plan = jnp.asarray(np.array(plan, np.int32).reshape(-1))
 
         into, back, blocks = modal_tables()
         tables = jnp.asarray(blocks, jnp.float32)
@@ -577,7 +581,13 @@
             in_specs=[smem, smem] + [vmem] * 11,
             out_specs=vmem,
             scratch_shapes=[
-                scratch((6 * slices + 10) * SIZE),
+                scratch((slices + 1) * SIZE),
+                scratch((slices + 1) * SIZE),
+                scratch(slices * SIZE),
+                scratch(slices * SIZE),
+                scratch((slices + 3) * SIZE),
+                scratch(slices * SIZE),
+                *[scratch(SIZE)] * 6,
                 scratch(SIZE),
                 scratch(3840),
                 pltpu.VMEM((2, 160, 480), jnp.bfloat16),

time: 150 us -> 81.3 us (0.54)
  Pallas kernels: 132 us -> 63.1 us
    pallas_call x1, Pallas kernels: 132 us -> 63.1 us  [local(): pl.pallas_call(lambda plan, where, *refs: whole_grid_kernel(slices, plan,...]
  transfers between devices with their start and end apart: 7 -> 7, of which waited for: 1 -> 1; matrix products, arithmetic and copies ran while one was open for 3% -> 6% of each run, Pallas kernels for 0% -> 0%
where the time goes in v1:
time: 81.3 us; the launch traced here: 80.8 us
  Pallas kernels  63.1 us (78%)
  local copies, waits for them, and re-layouts  6.39 us (8%)
  starting transfers between devices  5.62 us (7%)
  waiting for transfers between devices  3.38 us (4%)
  other arithmetic  2.15 us (3%)
    pallas_call x1, Pallas kernels, local(): pl.pallas_call(lambda plan, where, *refs: whole_grid_kernel(slices, plan,...  63.1 us
    ppermute x3, starting transfers between devices, local(): near.append(lax.ppermute(block, 'sy', [(i, i ^ k) for i in range(4)]))  4.54 us
    ppermute x3, waiting for transfers between devices, local(): near.append(lax.ppermute(block, 'sy', [(i, i ^ k) for i in range(4)]))  3.37 us
    unnamed x21, local copies, waits for them, and re-layouts  2.49 us
    mul x13, local copies, waits for them, and re-layouts, local(): flux_jacobian[d][None, :, None, :, None] * tables[:, d, None, :, None, :]  1.82 us
  transfers between devices with their start and end apart: 7, of which 1 were waited for; matrix products, arithmetic and copies ran while one was open for 6% of the time, Pallas kernels for 0%

profile of v1, /device:TPU:0, one launch (start us, length us, event | category | flops | bytes accessed | tf_op | source)
XLA Modules:
  0.0 80.8 jit_solution(18381812347632847186)
XLA Ops:
  0.0 0.7 broadcast_in_dim.8
  0.7 0.9 %pad_maximum_fusion.1.refs_0_ = f32[328,128]{1,0:T(8,128)S(1)} fusion(f32[8,128]{1,0:T(8,128)S(1)} %broadcast_in_dim.8, f32[320,128]{1,0:T(8,128)} %bitcast.21), kind=kLoop, calls=%fused_computation.2 | loop fusion | flops 41984 | bytes 335872 | tf_op jit(solution)/shard_map/concatenate | solution.py:551
  1.6 0.0 copy-start
  1.6 3.0 %collective-permute-start = (f32[328,128]{1,0:T(8,128)S(1)}, f32[328,128]{1,0:T(8,128)S(1)}, u32[]{:S(2)}, u32[]{:S(2)}) collective-permute-start(f32[328,128]{1,0:T(8,128)S(1)} %pad_maximum_fusion.1.refs_0_), channel_id=1, source_target_pairs={{0,1},{1,0},{2,3},{3,2},{4,5},{5,4},{6,7},{7,6},{8,9},{9,8},{10,11... | collective-permute-start | bytes 503816 | tf_op jit(solution)/shard_map/ppermute | solution.py:556
  4.6 1.5 %collective-permute-start.1 = (f32[328,128]{1,0:T(8,128)S(1)}, f32[328,128]{1,0:T(8,128)S(1)}, u32[]{:S(2)}, u32[]{:S(2)}) collective-permute-start(f32[328,128]{1,0:T(8,128)S(1)} %pad_maximum_fusion.1.refs_0_), channel_id=1, source_target_pairs={{0,2},{1,3},{2,0},{3,1},{4,6},{5,7},{6,4},{7,5},{8,10},{9,11},{10,... | collective-permute-start | bytes 503816 | tf_op jit(solution)/shard_map/ppermute | solution.py:556
  6.1 0.0 collective-permute-start.2
  6.1 0.0 collective-permute-start.3
  6.1 0.8 %fusion = (f32[1,5,5]{2,0,1:T(1,128)S(1)}, f32[1,5,5]{2,0,1:T(1,128)S(1)}, f32[1,5,5]{2,0,1:T(1,128)S(1)}) fusion(f32[3,5,5]{2,0,1:T(4,128)} %param.9), kind=kLoop, calls=%fused_computation.6 | loop fusion | bytes 600 | tf_op jit(solution)/shard_map/slice | solution.py:568
  7.0 0.1 mul.104
  7.1 0.1 mul.105
  7.2 0.1 mul.96
  7.3 0.0 copy-start.8
  7.4 0.1 mul.97
  7.5 0.0 copy-done
  7.5 0.1 mul.88
  7.6 0.1 mul.89
  7.8 0.3 copy-done.8
  8.1 0.0 copy-start.9
  8.1 0.1 mul.100
  8.2 0.3 mul.101
  8.5 0.4 copy-done.9
  8.9 0.0 copy-start.7
  8.9 0.1 mul.108
  9.0 0.3 mul.109
  9.2 0.4 copy-done.7
  9.6 0.1 mul.92
  9.7 0.3 mul.93
  10.0 0.0 collective-permute-done.refs_1_
  10.0 0.0 copy-start.1
  10.0 0.6 collective-permute-start.4
  10.6 3.4 %collective-permute-done.1.refs_2_ = f32[328,128]{1,0:T(8,128)S(1)} collective-permute-done((f32[328,128]{1,0:T(8,128)S(1)}, f32[328,128]{1,0:T(8,128)S(1)}, u32[]{:S(2)}, u32[]{:S(2)}) %collective-permute-start.1) | collective-permute-done | bytes 167968 | tf_op jit(solution)/shard_map/ppermute | solution.py:556
  13.9 0.0 copy-start.2
  13.9 0.0 collective-permute-start.5
  14.0 0.0 collective-permute-done.2.refs_3_
  14.0 0.0 copy-start.3
  14.0 0.5 collective-permute-start.6
  14.5 0.1 multiply_add_fusion
  14.6 0.6 stack.40.where
  15.2 1.1 %pad_maximum_fusion.refs_8_ = f32[2,160,480]{2,1,0:T(8,128)} fusion(f32[2,160,160]{2,1,0:T(8,128)S(1)} %multiply_add_fusion), kind=kLoop, calls=%fused_computation | loop fusion | flops 307200 | bytes 819200 | tf_op jit(solution)/shard_map/concatenate | solution.py:570
  16.3 0.0 copy-done.1
  16.3 0.0 copy-done.2
  16.3 0.0 copy-done.3
  16.3 0.0 collective-permute-done.3.refs_4_
  16.3 0.0 collective-permute-done.4.refs_5_
  16.3 0.0 copy-start.4
  16.3 0.0 collective-permute-done.5.refs_6_
  16.4 0.0 copy-start.5
  16.4 0.0 collective-permute-done.6.refs_7_
  16.4 0.6 copy-done.4
  17.0 0.1 copy-done.5
  17.1 0.0 copy-start.6
  17.1 0.7 copy-done.6
  17.7 63.1 %shard_map.73 = f32[3,320,128]{2,1,0:T(8,128)} custom-call(s32[195]{0:T(256)} %constant.28.clone.plan, s32[10]{0:T(128)} %stack.40.where, f32[328,128]{1,0:T(8,128)} %copy-done, f32[328,128]{1,0:T(8,128)} %copy-done.1, f32[328,128]{1,0:T(8,128)} %copy-done.2, f32[328,128]{1,0:T(8,128)} %copy-done.3, f32[328,128]{1,0:T(8,128)} %collective-permute-done.3.refs_4_, ...), custom_call_target="tpu_custom_call" | custom-call | tf_op jit(solution)/shard_map/pallas_call | solution.py:578
  (2 shorter events, 0.0 us)
Async XLA Ops:
  1.6 5.9 %copy-start = (f32[328,128]{1,0:T(8,128)}, f32[328,128]{1,0:T(8,128)S(1)}, u32[]{:S(2)}) copy-start(f32[328,128]{1,0:T(8,128)S(1)} %pad_maximum_fusion.1.refs_0_) | copy-start | bytes 503812
  1.6 8.4 %collective-permute-start = (f32[328,128]{1,0:T(8,128)S(1)}, f32[328,128]{1,0:T(8,128)S(1)}, u32[]{:S(2)}, u32[]{:S(2)}) collective-permute-start(f32[328,128]{1,0:T(8,128)S(1)} %pad_maximum_fusion.1.refs_0_), channel_id=1, source_target_pairs={{0,1},{1,0},{2,3},{3,2},{4,5},{5,4},{6,7},{7,6},{8,9},{9,8},{10,11... | collective-permute-start | bytes 503816 | tf_op jit(solution)/shard_map/ppermute | solution.py:556
  4.6 9.3 %collective-permute-start.1 = (f32[328,128]{1,0:T(8,128)S(1)}, f32[328,128]{1,0:T(8,128)S(1)}, u32[]{:S(2)}, u32[]{:S(2)}) collective-permute-start(f32[328,128]{1,0:T(8,128)S(1)} %pad_maximum_fusion.1.refs_0_), channel_id=1, source_target_pairs={{0,2},{1,3},{2,0},{3,1},{4,6},{5,7},{6,4},{7,5},{8,10},{9,11},{10,... | collective-permute-start | bytes 503816 | tf_op jit(solution)/shard_map/ppermute | solution.py:556
  6.1 7.8 %collective-permute-start.2 = (f32[328,128]{1,0:T(8,128)S(1)}, f32[328,128]{1,0:T(8,128)S(1)}, u32[]{:S(2)}, u32[]{:S(2)}) collective-permute-start(f32[328,128]{1,0:T(8,128)S(1)} %pad_maximum_fusion.1.refs_0_), channel_id=1, source_target_pairs={{0,3},{1,2},{2,1},{3,0},{4,7},{5,6},{6,5},{7,4},{8,11},{9,10},{10,... | collective-permute-start | bytes 503816 | tf_op jit(solution)/shard_map/ppermute | solution.py:556
  6.1 10.2 %collective-permute-start.3 = (f32[328,128]{1,0:T(8,128)S(1)}, f32[328,128]{1,0:T(8,128)}, u32[]{:S(2)}, u32[]{:S(2)}) collective-permute-start(f32[328,128]{1,0:T(8,128)S(1)} %pad_maximum_fusion.1.refs_0_), channel_id=1, source_target_pairs={{0,4},{4,0},{1,5},{5,1},{2,6},{6,2},{3,7},{7,3},{8,12},{12,8},{9,1... | collective-permute-start | bytes 503816 | tf_op jit(solution)/shard_map/ppermute | solution.py:557
  7.3 0.8 copy-start.8
  8.1 0.8 copy-start.9
  8.9 0.8 copy-start.7
  10.0 6.3 %copy-start.1 = (f32[328,128]{1,0:T(8,128)}, f32[328,128]{1,0:T(8,128)S(1)}, u32[]{:S(2)}) copy-start(f32[328,128]{1,0:T(8,128)S(1)} %collective-permute-done.refs_1_) | copy-start | bytes 503812
  10.0 6.3 %collective-permute-start.4 = (f32[328,128]{1,0:T(8,128)S(1)}, f32[328,128]{1,0:T(8,128)S(1)}, u32[]{:S(2)}, u32[]{:S(2)}) collective-permute-start(f32[328,128]{1,0:T(8,128)S(1)} %collective-permute-done.refs_1_), channel_id=1, source_target_pairs={{0,4},{4,0},{1,5},{5,1},{2,6},{6,2},{3,7},{7,3},{8,12},{12,8},{9,1... | collective-permute-start | bytes 503816 | tf_op jit(solution)/shard_map/ppermute | solution.py:557
  13.9 2.4 %copy-start.2 = (f32[328,128]{1,0:T(8,128)}, f32[328,128]{1,0:T(8,128)S(1)}, u32[]{:S(2)}) copy-start(f32[328,128]{1,0:T(8,128)S(1)} %collective-permute-done.1.refs_2_) | copy-start | bytes 503812
  13.9 2.4 %collective-permute-start.5 = (f32[328,128]{1,0:T(8,128)S(1)}, f32[328,128]{1,0:T(8,128)S(1)}, u32[]{:S(2)}, u32[]{:S(2)}) collective-permute-start(f32[328,128]{1,0:T(8,128)S(1)} %collective-permute-done.1.refs_2_), channel_id=1, source_target_pairs={{0,4},{4,0},{1,5},{5,1},{2,6},{6,2},{3,7},{7,3},{8,12},{12,8},{9,1... | collective-permute-start | bytes 503816 | tf_op jit(solution)/shard_map/ppermute | solution.py:557
  14.0 2.4 %copy-start.3 = (f32[328,128]{1,0:T(8,128)}, f32[328,128]{1,0:T(8,128)S(1)}, u32[]{:S(2)}) copy-start(f32[328,128]{1,0:T(8,128)S(1)} %collective-permute-done.2.refs_3_) | copy-start | bytes 503812
  14.0 2.4 %collective-permute-start.6 = (f32[328,128]{1,0:T(8,128)S(1)}, f32[328,128]{1,0:T(8,128)S(1)}, u32[]{:S(2)}, u32[]{:S(2)}) collective-permute-start(f32[328,128]{1,0:T(8,128)S(1)} %collective-permute-done.2.refs_3_), channel_id=1, source_target_pairs={{0,4},{4,0},{1,5},{5,1},{2,6},{6,2},{3,7},{7,3},{8,12},{12,8},{9,1... | collective-permute-start | bytes 503816 | tf_op jit(solution)/shard_map/ppermute | solution.py:557
  16.3 0.7 copy-start.4
  16.4 0.7 copy-start.5
  17.1 0.7 copy-start.6

commit v2 on v1

--- a/solution.py
+++ b/solution.py
@@ -248,6 +248,9 @@
     return jnp.concatenate([high, high, low], axis=0)
 
 
+ORDER = [9, 8, 7, 10, 11, 12, 13, 0, 1, 2, 3, 4, 5, 6]
+
+
 def steps(slices):
     work, mid, copy = slices, slices + 1, slices + 2
     plan = [(0, work, 0), (1, work, 0), (2, work, 0), (3, work, 0), (4, work, 0), (5, work, 0)]
@@ -261,34 +264,41 @@
     return plan
 
 
-def whole_grid_kernel(slices, plan, where, *refs):
+def whole_grid_kernel(slices, plan, *refs):
     gathered, refs = refs[:8], refs[8:]
     matrix, into, back, out, *refs = refs
-    ss, gg, tt, pp, vv, uu, first, quad, base, zed, c0, hga, tr, g, m, dh, dd, el, cc = refs
+    ss, gg, tt, pp, vv, uu, first, quad, base, zed, c0, hga, c2, tr, g, m, dh, dd, de, el, cc, gin, sems = refs
     f32 = jnp.float32
     work, mid, copy = slices * SIZE, (slices + 1) * SIZE, (slices + 2) * SIZE
 
+    copies = [pltpu.make_async_copy(gathered[k], gin.at[k], sems.at[k]) for k in range(8)]
+    for copy_in in copies:
+        copy_in.start()
+    x_here, y_here = lax.axis_index("sx"), lax.axis_index("sy")
+    mine, column = lax.axis_index("tm"), 4 * x_here + y_here
+    places = [(x_here ^ (k // 4)) * 4 + (y_here ^ (k % 4)) for k in range(8)]
+    for p in range(2):
+        whole = matrix[p]
+        high = whole.astype(jnp.bfloat16).astype(f32)
+        m[p] = jnp.concatenate([high, whole - high, high], axis=1).astype(jnp.bfloat16)
+    for copy_in in copies:
+        copy_in.wait()
     for k in range(8):
-        cc[pl.ds(where[2 + k], 1), :] = gathered[k][320:321, :]
+        cc[pl.ds(places[k], 1), :] = gin[k, 320:321, :]
     visc = cc[...]
     for i, levels in enumerate(LEVELS):
         lam = (HALF_STEP * eigen(levels)) * visc
         el[8 * i : 8 * i + 8, :] = lam
         dh[8 * i : 8 * i + 8, :] = 1.0 / (1.0 + lam)
         dd[8 * i : 8 * i + 8, :] = 1.0 / (1.0 + 2.0 * lam)
-    for p in range(2):
-        whole = matrix[p]
-        high = whole.astype(jnp.bfloat16).astype(f32)
-        lane = lax.broadcasted_iota(jnp.int32, whole.shape, 1)
-        middle = (lane >= 160) & (lane < 320)
-        m[p] = jnp.where(middle, whole - high, high).astype(jnp.bfloat16)
+        de[8 * i : 8 * i + 8, :] = 2.0 / (1.0 + 2.0 * lam)
     for k in range(0, 8, 2):
         for f in range(FIELDS):
-            x = jnp.concatenate([gathered[k + i][64 * f : 64 * f + 64, :] for i in (0, 1)], axis=1)
+            x = jnp.concatenate([gin[k + i, 64 * f : 64 * f + 64, :] for i in (0, 1)], axis=1)
             r = jnp.dot(into[...], split_rows(x), preferred_element_type=f32)
             for i in (0, 1):
                 for p in (0, 1):
-                    at = p * 1280 + f * 256 + where[2 + k + i]
+                    at = p * 1280 + f * 256 + places[k + i]
                     part = r[32 * p : 32 * p + 32, 128 * i : 128 * i + 128]
                     ss[pl.ds(at, 32, 8), :] = part
                     vv[pl.ds(work + at, 32, 8), :] = part
@@ -296,19 +306,21 @@
     sub = lax.broadcasted_iota(jnp.int32, (8, 128), 0)
     lane = lax.broadcasted_iota(jnp.int32, (8, 128), 1)
     tau = jnp.where(sub >= 4, 1.0, -1.0).astype(f32)
+    tau_1, tau_3 = PICK_1 * tau, PICK_3 * tau
     y_first, y_last = sub % 4 == 0, sub % 4 == 3
     z_first, z_last = lane == 0, lane == 127
     scaled = (HALF_STEP * BETA * 0.25) * visc
 
     def transport(at):
-        for jp in range(4):
+        for half in range(2):
             for p in range(2):
-                begin = at + (p * 1280 + 2 * jp)
-                x = jnp.concatenate([vv[pl.ds(begin + i, 160, 8), :] for i in (0, 1)], axis=1)
+                begin = at + (p * 1280 + 4 * half)
+                x = jnp.concatenate([vv[pl.ds(begin + i, 160, 8), :] for i in range(4)], axis=1)
                 r = jnp.dot(m[p], split_rows(x), preferred_element_type=f32)
-                for i in (0, 1):
-                    tr[pl.ds((1 - p) * 1280 + 2 * jp + i, 160, 8), :] = r[:, 128 * i : 128 * i + 128]
-            yield
+                for i in range(4):
+                    row = (1 - p) * 1280 + 4 * half + i
+                    tr[pl.ds(row, 160, 8), :] = r[:, 128 * i : 128 * i + 128]
+                yield
 
     def faces(at_x, at_y, at_z):
         def ld(at, a, b, c):
@@ -319,8 +331,8 @@
                 for q in range(4):
                     i = 8 * (16 * f + 4 * p + q)
                     even = ld(at_x, 0, p, q) + ld(at_x, 2, p, q)
-                    odd = PICK_1 * ld(at_x, 1, p, q) + PICK_3 * ld(at_x, 3, p, q)
-                    met = pltpu.roll(even + tau * odd, 4, 0)
+                    odd = tau_1 * ld(at_x, 1, p, q) + tau_3 * ld(at_x, 3, p, q)
+                    met = pltpu.roll(even + odd, 4, 0)
                     g[i : i + 8, :] = met
                     g[640 + i : 648 + i, :] = tau * met
                     even = ld(at_y, p, 0, q) + ld(at_y, p, 2, q)
@@ -410,11 +422,11 @@
             u2 = tab(dh, i) * (u1 - image)
             start = ld(ss, row)
             put(vv, row, u1 - 0.5 * (start + u2), 0, mid)
-            put(vv, row, (4.0 / 3.0) * u1 + (1.0 / 3.0) * u2, 0, work)
-            q = (5.0 / 6.0) * u2 - (2.0 / 3.0) * u1
+            mix = (4.0 / 3.0) * u1 + (1.0 / 3.0) * u2
+            put(vv, row, mix, 0, work)
+            q = u2 + u2 - mix
             put(quad, row, q)
-            lam = tab(el, i)
-            put(base, row, lam * (2.0 * q - (1.0 / 3.0) * start) - (1.0 / 3.0) * ld(gg, row))
+            put(base, row, tab(el, i) * (q - (1.0 / 3.0) * start) - (1.0 / 3.0) * ld(gg, row))
 
         finish(store)
 
@@ -422,14 +434,16 @@
         def store(row, i, image):
             z = ld(base, row) - image
             put(zed, row, z)
-            put(vv, row, 2.0 * (tab(dd, i) * (ld(ss, row) + z) - ld(quad, row)), 0, work)
+            put(vv, row, tab(de, i) * (ld(ss, row) + z) - ld(quad, row), 0, work)
 
         finish(store)
 
     def kind_6(t):
         def store(row, i, image):
             put(hga, row, image)
-            put(c0, row, (1.0 / 3.0) * (tab(el, i) * ld(vv, row, 0, mid) + image))
+            c = (1.0 / 3.0) * (tab(el, i) * ld(vv, row, 0, mid) + image)
+            put(c0, row, c)
+            put(c2, row, c + c)
 
         finish(store)
 
@@ -440,7 +454,7 @@
             s = tab(dd, i) * (ld(ss, row, at) + ld(base, row) - image)
             put(ss, row, s, at, SIZE)
             put(vv, row, s, 0, copy)
-            put(vv, row, 2.0 * (tab(dd, i) * (s + ld(zed, row)) - ld(quad, row)), 0, work)
+            put(vv, row, tab(de, i) * (s + ld(zed, row)) - ld(quad, row), 0, work)
 
         finish(store)
 
@@ -452,10 +466,9 @@
             s = ld(ss, row, at)
             old = ld(gg, row, at)
             phi = 0.25 * (tab(el, i) * (ld(ss, row, at, SIZE) - s) + image - old)
-            c = ld(c0, row)
-            target = s + phi + c
+            target = s + phi + ld(c0, row)
             put(tt, row, target, at)
-            put(pp, row, phi - 2.0 * c, at)
+            put(pp, row, phi - ld(c2, row), at)
             put(vv, row, tab(dh, i) * (target - ld(hga, row) - 0.5 * (old + image)), at)
 
         finish(store)
@@ -487,12 +500,13 @@
             u1 = ld(uu, row, at)
             u2 = tab(dh, i) * (ld(tt, row, at) - image)
             s = ld(ss, row, at)
-            q = (5.0 / 6.0) * u2 - (2.0 / 3.0) * u1
+            mix = (4.0 / 3.0) * u1 + (1.0 / 3.0) * u2
+            put(vv, row, mix, at)
+            q = u2 + u2 - mix
             put(pp, row, q, at)
-            put(vv, row, (4.0 / 3.0) * u1 + (1.0 / 3.0) * u2, at)
             put(uu, row, u1 - 0.5 * (s + u2), at)
             old = ld(gg, row, at)
-            put(tt, row, tab(el, i) * (2.0 * q - (1.0 / 3.0) * s) - (1.0 / 3.0) * old, at)
+            put(tt, row, tab(el, i) * (q - (1.0 / 3.0) * s) - (1.0 / 3.0) * old, at)
 
         finish(store)
 
@@ -502,7 +516,7 @@
         def store(row, i, image):
             z = ld(tt, row, at) - image
             put(gg, row, z, at)
-            put(vv, row, 2.0 * (tab(dd, i) * (ld(ss, row) + z) - ld(pp, row, at)), 0, work)
+            put(vv, row, tab(de, i) * (ld(ss, row) + z) - ld(pp, row, at), 0, work)
 
         finish(store)
 
@@ -514,12 +528,12 @@
             s = tab(dd, i) * (ld(ss, row, at) + ld(tt, row, at) - image)
             put(ss, row, s, at, SIZE)
             z = ld(gg, row, later)
-            put(vv, row, 2.0 * (tab(dd, i) * (s + z) - ld(pp, row, later)), 0, work)
-
-        finish(store)
-
-    kinds = [kind_0, kind_1, kind_2, kind_3, kind_4, kind_5, kind_6, kind_7, kind_8, kind_9]
-    kinds += [kind_10, kind_11, kind_12, kind_13]
+            put(vv, row, tab(de, i) * (s + z) - ld(pp, row, later), 0, work)
+
+        finish(store)
+
+    kinds = [kind_9, kind_8, kind_7, kind_10, kind_11, kind_12, kind_13]
+    kinds += [kind_0, kind_1, kind_2, kind_3, kind_4, kind_5, kind_6]
 
     def step(n, carry):
         at = [pl.multiple_of(plan[5 * n + i], SIZE) for i in range(1, 4)]
@@ -531,7 +545,6 @@
 
     lax.fori_loop(0, len(steps(slices)), step, 0)
 
-    mine, column = where[0], where[1]
     for f in range(FIELDS):
 
         def own(ref, slot):
@@ -546,20 +559,26 @@
             out[i, 64 * f : 64 * f + 64, :] = r[:, 128 * i : 128 * i + 128]
 
 
+def join_kernel(values, viscosity, out):
+    out[0:ROWS, :] = values[...]
+    out[ROWS : ROWS + 8, :] = jnp.broadcast_to(viscosity[...], (8, 128))
+
+
 def local_whole_grid(slices):
     def local(initial, viscosity, flux_jacobian):
-        block = jnp.concatenate(
-            [initial.reshape(ROWS, 128), jnp.broadcast_to(viscosity.reshape(1, 128), (8, 128))], axis=0
-        )
+        vmem = pl.BlockSpec(memory_space=pltpu.VMEM)
+        block = pl.pallas_call(
+            join_kernel,
+            out_shape=jax.ShapeDtypeStruct((ROWS + 8, 128), jnp.float32),
+            in_specs=[vmem, vmem],
+            out_specs=vmem,
+        )(initial.reshape(ROWS, 128), viscosity.reshape(1, 128))
         near = [block]
         for k in range(1, 4):
             near.append(lax.ppermute(block, "sy", [(i, i ^ k) for i in range(4)]))
         gathered = near + [lax.ppermute(b, "sx", [(0, 1), (1, 0)]) for b in near]
 
-        x, y = lax.axis_index("sx"), lax.axis_index("sy")
-        columns = [(x ^ (k // 4)) * 4 + (y ^ (k % 4)) for k in range(8)]
-        where = jnp.stack([lax.axis_index("tm"), x * 4 + y] + columns).astype(jnp.int32)
-        plan = [(kind, at * SIZE, at * SIZE, at * SIZE, t) for kind, at, t in steps(slices)]
+        plan = [(ORDER.index(kind), at * SIZE, at * SIZE, at * SIZE, t) for kind, at, t in steps(slices)]
         plan = jnp.asarray(np.array(plan, np.int32).reshape(-1))
 
         into, back, blocks = modal_tables()
@@ -567,18 +586,17 @@
         matrix = sum(
             flux_jacobian[d][None, :, None, :, None] * tables[:, d, None, :, None, :] for d in range(3)
         ).reshape(2, 160, 160)
-        matrix = jnp.concatenate([matrix, matrix, matrix], axis=2)
 
         smem = pl.BlockSpec(memory_space=pltpu.SMEM)
-        vmem = pl.BlockSpec(memory_space=pltpu.VMEM)
+        anywhere = pl.BlockSpec(memory_space=pl.ANY)
 
         def scratch(rows):
             return pltpu.VMEM((rows, 128), jnp.float32)
 
         out = pl.pallas_call(
-            lambda plan, where, *refs: whole_grid_kernel(slices, plan, where, *refs),
+            lambda plan, *refs: whole_grid_kernel(slices, plan, *refs),
             out_shape=jax.ShapeDtypeStruct((3, ROWS, 128), jnp.float32),
-            in_specs=[smem, smem] + [vmem] * 11,
+            in_specs=[smem] + [anywhere] * 8 + [vmem] * 3,
             out_specs=vmem,
             scratch_shapes=[
                 scratch((slices + 1) * SIZE),
@@ -587,17 +605,17 @@
                 scratch(slices * SIZE),
                 scratch((slices + 3) * SIZE),
                 scratch(slices * SIZE),
-                *[scratch(SIZE)] * 6,
+                *[scratch(SIZE)] * 7,
                 scratch(SIZE),
                 scratch(3840),
                 pltpu.VMEM((2, 160, 480), jnp.bfloat16),
-                scratch(8 * len(LEVELS)),
-                scratch(8 * len(LEVELS)),
-                scratch(8 * len(LEVELS)),
+                *[scratch(8 * len(LEVELS))] * 4,
                 scratch(8),
+                pltpu.VMEM((8, ROWS + 8, 128), jnp.float32),
+                pltpu.SemaphoreType.DMA((8,)),
             ],
             compiler_params=pltpu.CompilerParams(vmem_limit_bytes=58 << 20),
-        )(plan, where, *gathered, matrix, three_pass(into), three_pass(back))
+        )(plan, *gathered, matrix, three_pass(into), three_pass(back))
         return out.reshape(1, 3, 1, 1, FIELDS, 64, 128)
 
     return local

time: 81.3 us -> 79.1 us (0.973)
  local copies, waits for them, and re-layouts: 6.39 us -> 4.97 us
  other arithmetic: 2.15 us -> 0.82 us
    concatenate x2 -> x0, other arithmetic: 2.05 us -> none  [the longest x1 1.12 us: local(): matrix = jnp.concatenate([matrix, matrix, matrix], axis=2)]
    pallas_call x1 -> x2, Pallas kernels: 63.1 us -> 63.3 us  [the longest x1 61.7 us: local(): pl.pallas_call(lambda plan, *refs: whole_grid_kernel(slices, plan, *refs)...]
  transfers between devices with their start and end apart: 7 -> 7, of which waited for: 1 -> 2; matrix products, arithmetic and copies ran while one was open for 6% -> 4% of each run, Pallas kernels for 0% -> 0%
where the time goes in v2:
time: 79.1 us; the launch traced here: 78.7 us
  Pallas kernels  63.3 us (80%)
  starting transfers between devices  5.53 us (7%)
  local copies, waits for them, and re-layouts  4.97 us (6%)
  waiting for transfers between devices  3.88 us (5%)
  other arithmetic  0.82 us (1%)
    pallas_call x1, Pallas kernels, local(): pl.pallas_call(lambda plan, *refs: whole_grid_kernel(slices, plan, *refs)...  61.7 us
    ppermute x3, starting transfers between devices, local(): near.append(lax.ppermute(block, 'sy', [(i, i ^ k) for i in range(4)]))  4.46 us
    ppermute x3, waiting for transfers between devices, local(): near.append(lax.ppermute(block, 'sy', [(i, i ^ k) for i in range(4)]))  3.59 us
    unnamed x21, local copies, waits for them, and re-layouts  2.32 us
    mul x13, local copies, waits for them, and re-layouts, local(): flux_jacobian[d][None, :, None, :, None] * tables[:, d, None, :, None, :]  1.82 us
    pallas_call x1, Pallas kernels, local(): pl.pallas_call(join_kernel, out_shape=jax.ShapeDtypeStruct((ROWS + 8, 128...  1.59 us
  transfers between devices with their start and end apart: 7, of which 2 were waited for; matrix products, arithmetic and copies ran while one was open for 4% of the time, Pallas kernels for 0%

profile of v2, /device:TPU:0, one launch (start us, length us, event | category | flops | bytes accessed | tf_op | source)
XLA Modules:
  0.0 78.7 jit_solution(14324030931409873077)
XLA Ops:
  0.0 1.6 %shard_map.73.refs_0_ = f32[328,128]{1,0:T(8,128)} custom-call(f32[320,128]{1,0:T(8,128)} %bitcast.12, f32[1,128]{1,0:T(1,128)} %bitcast.14), custom_call_target="tpu_custom_call" | custom-call | tf_op jit(solution)/shard_map/pallas_call | solution.py:570
  1.6 2.9 %collective-permute-start = (f32[328,128]{1,0:T(8,128)}, f32[328,128]{1,0:T(8,128)S(1)}, u32[]{:S(2)}, u32[]{:S(2)}) collective-permute-start(f32[328,128]{1,0:T(8,128)} %shard_map.73.refs_0_), channel_id=1, source_target_pairs={{0,1},{1,0},{2,3},{3,2},{4,5},{5,4},{6,7},{7,6},{8,9},{9,8},{10,11... | collective-permute-start | bytes 503816 | tf_op jit(solution)/shard_map/ppermute | solution.py:578
  4.5 1.5 %collective-permute-start.1 = (f32[328,128]{1,0:T(8,128)}, f32[328,128]{1,0:T(8,128)S(1)}, u32[]{:S(2)}, u32[]{:S(2)}) collective-permute-start(f32[328,128]{1,0:T(8,128)} %shard_map.73.refs_0_), channel_id=1, source_target_pairs={{0,2},{1,3},{2,0},{3,1},{4,6},{5,7},{6,4},{7,5},{8,10},{9,11},{10,... | collective-permute-start | bytes 503816 | tf_op jit(solution)/shard_map/ppermute | solution.py:578
  6.1 0.0 collective-permute-start.2
  6.1 0.0 collective-permute-start.3
  6.1 0.8 %fusion = (f32[1,5,5]{2,0,1:T(1,128)S(1)}, f32[1,5,5]{2,0,1:T(1,128)S(1)}, f32[1,5,5]{2,0,1:T(1,128)S(1)}) fusion(f32[3,5,5]{2,0,1:T(4,128)} %param.9), kind=kLoop, calls=%fused_computation.4 | loop fusion | bytes 600 | tf_op jit(solution)/shard_map/slice | solution.py:587
  6.9 0.1 mul.81
  7.0 0.1 mul.82
  7.1 0.1 mul.89
  7.3 0.0 copy-start.8
  7.3 0.1 mul.90
  7.4 0.1 mul.73
  7.5 0.1 mul.74
  7.7 0.4 copy-done.8
  8.0 0.0 copy-start.9
  8.0 0.1 mul.77
  8.1 0.3 mul.78
  8.4 0.4 copy-done.9
  8.8 0.0 copy-start.7
  8.8 0.1 mul.85
  8.9 0.3 mul.86
  9.1 0.4 copy-done.7
  9.5 0.1 mul.93
  9.6 0.3 mul.94
  9.9 0.0 collective-permute-done.refs_1_
  9.9 0.0 copy-start
  9.9 0.6 collective-permute-start.4
  10.5 3.6 %collective-permute-done.1.refs_2_ = f32[328,128]{1,0:T(8,128)S(1)} collective-permute-done((f32[328,128]{1,0:T(8,128)}, f32[328,128]{1,0:T(8,128)S(1)}, u32[]{:S(2)}, u32[]{:S(2)}) %collective-permute-start.1) | collective-permute-done | bytes 167968 | tf_op jit(solution)/shard_map/ppermute | solution.py:578
  14.1 0.0 copy-start.1
  14.1 0.0 collective-permute-start.5
  14.1 0.0 collective-permute-done.2.refs_3_
  14.1 0.0 copy-start.2
  14.1 0.5 collective-permute-start.6
  14.6 0.8 %multiply_add_fusion.refs_8_ = f32[2,160,160]{2,1,0:T(8,128)} fusion(f32[2,160,160]{2,1,0:T(8,128)S(1)} %mul.94, f32[2,160,160]{2,1,0:T(8,128)S(1)} %mul.86, f32[2,160,160]{2,1,0:T(8,128)S(1)} %mul.78, f32[160,160]{1,0:T(8,128)S(1)} %mul.90, f32[160,160]{1,0:T(8,128)S(1)} %mul.82, f32[160,160]{1,0:T(8,128)S(1)} %mul.74), kind=kLoop, calls=%fused_computation | loop fusion | flops 256000 | bytes 1126400 | tf_op jit(solution)/shard_map/add | solution.py:586
  15.4 0.0 collective-permute-done.3.refs_4_
  15.4 0.0 copy-start.3
  15.4 0.0 collective-permute-done.4.refs_5_
  15.4 0.0 copy-start.4
  15.4 0.0 collective-permute-done.5.refs_6_
  15.5 0.0 copy-start.5
  15.5 0.2 collective-permute-done.6.refs_7_
  15.7 0.0 copy-done
  15.7 0.0 copy-done.1
  15.7 0.0 copy-done.2
  15.7 0.4 copy-done.3
  16.1 0.1 copy-done.4
  16.2 0.1 copy-done.5
  16.2 0.0 copy-start.6
  16.3 0.7 copy-done.6
  16.9 61.7 %shard_map.74 = f32[3,320,128]{2,1,0:T(8,128)} custom-call(s32[195]{0:T(256)} %constant.8.clone.plan, f32[328,128]{1,0:T(8,128)} %shard_map.73.refs_0_, f32[328,128]{1,0:T(8,128)} %copy-done, f32[328,128]{1,0:T(8,128)} %copy-done.1, f32[328,128]{1,0:T(8,128)} %copy-done.2, f32[328,128]{1,0:T(8,128)} %copy-done.3, f32[328,128]{1,0:T(8,128)} %copy-done.4, ...), custom_call_target="tpu_custom_call" | custom-call | tf_op jit(solution)/shard_map/pallas_call | solution.py:596
  (2 shorter events, 0.0 us)
Async XLA Ops:
  1.6 8.3 %collective-permute-start = (f32[328,128]{1,0:T(8,128)}, f32[328,128]{1,0:T(8,128)S(1)}, u32[]{:S(2)}, u32[]{:S(2)}) collective-permute-start(f32[328,128]{1,0:T(8,128)} %shard_map.73.refs_0_), channel_id=1, source_target_pairs={{0,1},{1,0},{2,3},{3,2},{4,5},{5,4},{6,7},{7,6},{8,9},{9,8},{10,11... | collective-permute-start | bytes 503816 | tf_op jit(solution)/shard_map/ppermute | solution.py:578
  4.5 9.6 %collective-permute-start.1 = (f32[328,128]{1,0:T(8,128)}, f32[328,128]{1,0:T(8,128)S(1)}, u32[]{:S(2)}, u32[]{:S(2)}) collective-permute-start(f32[328,128]{1,0:T(8,128)} %shard_map.73.refs_0_), channel_id=1, source_target_pairs={{0,2},{1,3},{2,0},{3,1},{4,6},{5,7},{6,4},{7,5},{8,10},{9,11},{10,... | collective-permute-start | bytes 503816 | tf_op jit(solution)/shard_map/ppermute | solution.py:578
  6.1 8.0 %collective-permute-start.2 = (f32[328,128]{1,0:T(8,128)}, f32[328,128]{1,0:T(8,128)S(1)}, u32[]{:S(2)}, u32[]{:S(2)}) collective-permute-start(f32[328,128]{1,0:T(8,128)} %shard_map.73.refs_0_), channel_id=1, source_target_pairs={{0,3},{1,2},{2,1},{3,0},{4,7},{5,6},{6,5},{7,4},{8,11},{9,10},{10,... | collective-permute-start | bytes 503816 | tf_op jit(solution)/shard_map/ppermute | solution.py:578
  6.1 9.4 %collective-permute-start.3 = (f32[328,128]{1,0:T(8,128)}, f32[328,128]{1,0:T(8,128)S(1)}, u32[]{:S(2)}, u32[]{:S(2)}) collective-permute-start(f32[328,128]{1,0:T(8,128)} %shard_map.73.refs_0_), channel_id=1, source_target_pairs={{0,4},{4,0},{1,5},{5,1},{2,6},{6,2},{3,7},{7,3},{8,12},{12,8},{9,1... | collective-permute-start | bytes 503816 | tf_op jit(solution)/shard_map/ppermute | solution.py:579
  7.3 0.8 copy-start.8
  8.0 0.8 copy-start.9
  8.8 0.8 copy-start.7
  9.9 5.8 %copy-start = (f32[328,128]{1,0:T(8,128)}, f32[328,128]{1,0:T(8,128)S(1)}, u32[]{:S(2)}) copy-start(f32[328,128]{1,0:T(8,128)S(1)} %collective-permute-done.refs_1_) | copy-start | bytes 503812
  9.9 5.5 %collective-permute-start.4 = (f32[328,128]{1,0:T(8,128)S(1)}, f32[328,128]{1,0:T(8,128)S(1)}, u32[]{:S(2)}, u32[]{:S(2)}) collective-permute-start(f32[328,128]{1,0:T(8,128)S(1)} %collective-permute-done.refs_1_), channel_id=1, source_target_pairs={{0,4},{4,0},{1,5},{5,1},{2,6},{6,2},{3,7},{7,3},{8,12},{12,8},{9,1... | collective-permute-start | bytes 503816 | tf_op jit(solution)/shard_map/ppermute | solution.py:579
  14.1 1.6 %copy-start.1 = (f32[328,128]{1,0:T(8,128)}, f32[328,128]{1,0:T(8,128)S(1)}, u32[]{:S(2)}) copy-start(f32[328,128]{1,0:T(8,128)S(1)} %collective-permute-done.1.refs_2_) | copy-start | bytes 503812
  14.1 1.4 %collective-permute-start.5 = (f32[328,128]{1,0:T(8,128)S(1)}, f32[328,128]{1,0:T(8,128)S(1)}, u32[]{:S(2)}, u32[]{:S(2)}) collective-permute-start(f32[328,128]{1,0:T(8,128)S(1)} %collective-permute-done.1.refs_2_), channel_id=1, source_target_pairs={{0,4},{4,0},{1,5},{5,1},{2,6},{6,2},{3,7},{7,3},{8,12},{12,8},{9,1... | collective-permute-start | bytes 503816 | tf_op jit(solution)/shard_map/ppermute | solution.py:579
  14.1 1.6 %copy-start.2 = (f32[328,128]{1,0:T(8,128)}, f32[328,128]{1,0:T(8,128)S(1)}, u32[]{:S(2)}) copy-start(f32[328,128]{1,0:T(8,128)S(1)} %collective-permute-done.2.refs_3_) | copy-start | bytes 503812
  14.1 1.6 %collective-permute-start.6 = (f32[328,128]{1,0:T(8,128)S(1)}, f32[328,128]{1,0:T(8,128)S(1)}, u32[]{:S(2)}, u32[]{:S(2)}) collective-permute-start(f32[328,128]{1,0:T(8,128)S(1)} %collective-permute-done.2.refs_3_), channel_id=1, source_target_pairs={{0,4},{4,0},{1,5},{5,1},{2,6},{6,2},{3,7},{7,3},{8,12},{12,8},{9,1... | collective-permute-start | bytes 503816 | tf_op jit(solution)/shard_map/ppermute | solution.py:579
  15.4 0.7 copy-start.3
  15.4 0.7 copy-start.4
  15.5 0.8 copy-start.5
  16.2 0.7 copy-start.6

commit v3 on v2

--- a/solution.py
+++ b/solution.py
@@ -392,7 +392,9 @@
     def kind_0(t):
         def store(row, i, image):
             put(gg, row, image)
-            put(vv, row, tab(dh, i) * (ld(ss, row) - image), 0, work)
+            start = ld(ss, row)
+            put(tt, row, start)
+            put(vv, row, tab(dh, i) * (start - image), 0, work)
 
         finish(store)
 
@@ -467,7 +469,7 @@
             old = ld(gg, row, at)
             phi = 0.25 * (tab(el, i) * (ld(ss, row, at, SIZE) - s) + image - old)
             target = s + phi + ld(c0, row)
-            put(tt, row, target, at)
+            put(tt, row, target, at, SIZE)
             put(pp, row, phi - ld(c2, row), at)
             put(vv, row, tab(dh, i) * (target - ld(hga, row) - 0.5 * (old + image)), at)
 
@@ -477,7 +479,7 @@
         at = t * SIZE
 
         def store(row, i, image):
-            put(vv, row, tab(dh, i) * (ld(tt, row, at) - image), at)
+            put(vv, row, tab(dh, i) * (ld(tt, row, at, SIZE) - image), at)
 
         finish(store)
 
@@ -485,10 +487,10 @@
         at = t * SIZE
 
         def store(row, i, image):
-            u = tab(dh, i) * (ld(tt, row, at) - image)
+            u = tab(dh, i) * (ld(tt, row, at, SIZE) - image)
             put(uu, row, u, at)
             target = u + ld(pp, row, at)
-            put(tt, row, target, at)
+            put(tt, row, target, at, SIZE)
             put(vv, row, tab(dh, i) * (target - ld(gg, row, at, SIZE)), at)
 
         finish(store)
@@ -498,15 +500,14 @@
 
         def store(row, i, image):
             u1 = ld(uu, row, at)
-            u2 = tab(dh, i) * (ld(tt, row, at) - image)
+            u2 = tab(dh, i) * (ld(tt, row, at, SIZE) - image)
             s = ld(ss, row, at)
             mix = (4.0 / 3.0) * u1 + (1.0 / 3.0) * u2
             put(vv, row, mix, at)
             q = u2 + u2 - mix
             put(pp, row, q, at)
-            put(uu, row, u1 - 0.5 * (s + u2), at)
             old = ld(gg, row, at)
-            put(tt, row, tab(el, i) * (q - (1.0 / 3.0) * s) - (1.0 / 3.0) * old, at)
+            put(tt, row, tab(el, i) * (q - (1.0 / 3.0) * s) - (1.0 / 3.0) * old, at, SIZE)
 
         finish(store)
 
@@ -514,7 +515,7 @@
         at = t * SIZE
 
         def store(row, i, image):
-            z = ld(tt, row, at) - image
+            z = ld(tt, row, at, SIZE) - image
             put(gg, row, z, at)
             put(vv, row, tab(de, i) * (ld(ss, row) + z) - ld(pp, row, at), 0, work)
 
@@ -525,8 +526,8 @@
         later = jnp.minimum(t + 1, slices - 1) * SIZE
 
         def store(row, i, image):
-            s = tab(dd, i) * (ld(ss, row, at) + ld(tt, row, at) - image)
-            put(ss, row, s, at, SIZE)
+            s = tab(dd, i) * (ld(tt, row, at) + ld(tt, row, at, SIZE) - image)
+            put(tt, row, s, at, SIZE)
             z = ld(gg, row, later)
             put(vv, row, tab(de, i) * (s + z) - ld(pp, row, later), 0, work)
 
@@ -551,8 +552,9 @@
             at = slot * SIZE + f * 256 + column
             return jnp.concatenate([ref[pl.ds(at + 1280 * p, 32, 8), :] for p in (0, 1)], axis=0)
 
-        begin, end = own(ss, mine), own(ss, mine + 1)
-        middle = own(uu, mine) + 0.5 * (begin + end)
+        begin, end = own(tt, mine), own(tt, mine + 1)
+        fine_end = 0.5 * (own(pp, mine) + own(vv, mine))
+        middle = own(uu, mine) + 0.5 * (begin - own(ss, mine) + end - fine_end)
         x = jnp.concatenate([begin, middle, end], axis=1)
         r = jnp.dot(back[...], split_rows(x), preferred_element_type=f32)
         for i in range(3):
@@ -588,7 +590,7 @@
         ).reshape(2, 160, 160)
 
         smem = pl.BlockSpec(memory_space=pltpu.SMEM)
-        anywhere = pl.BlockSpec(memory_space=pl.ANY)
+        hbm = pl.BlockSpec(memory_space=pltpu.HBM)
 
         def scratch(rows):
             return pltpu.VMEM((rows, 128), jnp.float32)
@@ -596,12 +598,12 @@
         out = pl.pallas_call(
             lambda plan, *refs: whole_grid_kernel(slices, plan, *refs),
             out_shape=jax.ShapeDtypeStruct((3, ROWS, 128), jnp.float32),
-            in_specs=[smem] + [anywhere] * 8 + [vmem] * 3,
+            in_specs=[smem] + [hbm] * 8 + [vmem] * 3,
             out_specs=vmem,
             scratch_shapes=[
                 scratch((slices + 1) * SIZE),
                 scratch((slices + 1) * SIZE),
-                scratch(slices * SIZE),
+                scratch((slices + 1) * SIZE),
                 scratch(slices * SIZE),
                 scratch((slices + 3) * SIZE),
                 scratch(slices * SIZE),

time: 79.1 us -> 78.7 us (level)
  no operation moved by 1% of the time
where the time goes in v3:
time: 78.7 us; the launch traced here: 78.3 us
  Pallas kernels  63 us (80%)
  starting transfers between devices  5.53 us (7%)
  local copies, waits for them, and re-layouts  4.97 us (6%)
  waiting for transfers between devices  3.88 us (5%)
  other arithmetic  0.82 us (1%)
    pallas_call x1, Pallas kernels, local(): pl.pallas_call(lambda plan, *refs: whole_grid_kernel(slices, plan, *refs)...  61.4 us
    ppermute x3, starting transfers between devices, local(): near.append(lax.ppermute(block, 'sy', [(i, i ^ k) for i in range(4)]))  4.46 us
    ppermute x3, waiting for transfers between devices, local(): near.append(lax.ppermute(block, 'sy', [(i, i ^ k) for i in range(4)]))  3.59 us
    unnamed x21, local copies, waits for them, and re-layouts  2.32 us
    mul x13, local copies, waits for them, and re-layouts, local(): flux_jacobian[d][None, :, None, :, None] * tables[:, d, None, :, None, :]  1.82 us
    pallas_call x1, Pallas kernels, local(): pl.pallas_call(join_kernel, out_shape=jax.ShapeDtypeStruct((ROWS + 8, 128...  1.59 us
  transfers between devices with their start and end apart: 7, of which 2 were waited for; matrix products, arithmetic and copies ran while one was open for 4% of the time, Pallas kernels for 0%

profile of v3, /device:TPU:0, one launch (start us, length us, event | category | flops | bytes accessed | tf_op | source)
XLA Modules:
  0.0 78.3 jit_solution(7145001207658844413)
XLA Ops:
  0.0 1.6 %shard_map.73.refs_0_ = f32[328,128]{1,0:T(8,128)} custom-call(f32[320,128]{1,0:T(8,128)} %bitcast.12, f32[1,128]{1,0:T(1,128)} %bitcast.14), custom_call_target="tpu_custom_call" | custom-call | tf_op jit(solution)/shard_map/pallas_call | solution.py:572
  1.6 2.9 %collective-permute-start = (f32[328,128]{1,0:T(8,128)}, f32[328,128]{1,0:T(8,128)S(1)}, u32[]{:S(2)}, u32[]{:S(2)}) collective-permute-start(f32[328,128]{1,0:T(8,128)} %shard_map.73.refs_0_), channel_id=1, source_target_pairs={{0,1},{1,0},{2,3},{3,2},{4,5},{5,4},{6,7},{7,6},{8,9},{9,8},{10,11... | collective-permute-start | bytes 503816 | tf_op jit(solution)/shard_map/ppermute | solution.py:580
  4.5 1.5 %collective-permute-start.1 = (f32[328,128]{1,0:T(8,128)}, f32[328,128]{1,0:T(8,128)S(1)}, u32[]{:S(2)}, u32[]{:S(2)}) collective-permute-start(f32[328,128]{1,0:T(8,128)} %shard_map.73.refs_0_), channel_id=1, source_target_pairs={{0,2},{1,3},{2,0},{3,1},{4,6},{5,7},{6,4},{7,5},{8,10},{9,11},{10,... | collective-permute-start | bytes 503816 | tf_op jit(solution)/shard_map/ppermute | solution.py:580
  6.1 0.0 collective-permute-start.2
  6.1 0.0 collective-permute-start.3
  6.1 0.8 %fusion = (f32[1,5,5]{2,0,1:T(1,128)S(1)}, f32[1,5,5]{2,0,1:T(1,128)S(1)}, f32[1,5,5]{2,0,1:T(1,128)S(1)}) fusion(f32[3,5,5]{2,0,1:T(4,128)} %param.9), kind=kLoop, calls=%fused_computation.4 | loop fusion | bytes 600 | tf_op jit(solution)/shard_map/slice | solution.py:589
  6.9 0.1 mul.81
  7.0 0.1 mul.82
  7.1 0.1 mul.89
  7.3 0.0 copy-start.8
  7.3 0.1 mul.90
  7.4 0.1 mul.73
  7.5 0.1 mul.74
  7.7 0.4 copy-done.8
  8.0 0.0 copy-start.9
  8.0 0.1 mul.77
  8.1 0.3 mul.78
  8.4 0.4 copy-done.9
  8.8 0.0 copy-start.7
  8.8 0.1 mul.85
  8.9 0.3 mul.86
  9.1 0.4 copy-done.7
  9.5 0.1 mul.93
  9.6 0.3 mul.94
  9.9 0.0 collective-permute-done.refs_1_
  9.9 0.0 copy-start
  9.9 0.6 collective-permute-start.4
  10.5 3.6 %collective-permute-done.1.refs_2_ = f32[328,128]{1,0:T(8,128)S(1)} collective-permute-done((f32[328,128]{1,0:T(8,128)}, f32[328,128]{1,0:T(8,128)S(1)}, u32[]{:S(2)}, u32[]{:S(2)}) %collective-permute-start.1) | collective-permute-done | bytes 167968 | tf_op jit(solution)/shard_map/ppermute | solution.py:580
  14.1 0.0 copy-start.1
  14.1 0.0 collective-permute-start.5
  14.1 0.0 collective-permute-done.2.refs_3_
  14.1 0.0 copy-start.2
  14.1 0.5 collective-permute-start.6
  14.6 0.8 %multiply_add_fusion.refs_8_ = f32[2,160,160]{2,1,0:T(8,128)} fusion(f32[2,160,160]{2,1,0:T(8,128)S(1)} %mul.94, f32[2,160,160]{2,1,0:T(8,128)S(1)} %mul.86, f32[2,160,160]{2,1,0:T(8,128)S(1)} %mul.78, f32[160,160]{1,0:T(8,128)S(1)} %mul.90, f32[160,160]{1,0:T(8,128)S(1)} %mul.82, f32[160,160]{1,0:T(8,128)S(1)} %mul.74), kind=kLoop, calls=%fused_computation | loop fusion | flops 256000 | bytes 1126400 | tf_op jit(solution)/shard_map/add | solution.py:588
  15.4 0.0 collective-permute-done.3.refs_4_
  15.4 0.0 copy-start.3
  15.4 0.0 collective-permute-done.4.refs_5_
  15.4 0.0 copy-start.4
  15.4 0.0 collective-permute-done.5.refs_6_
  15.5 0.0 copy-start.5
  15.5 0.2 collective-permute-done.6.refs_7_
  15.7 0.0 copy-done
  15.7 0.0 copy-done.1
  15.7 0.0 copy-done.2
  15.7 0.4 copy-done.3
  16.1 0.1 copy-done.4
  16.2 0.1 copy-done.5
  16.2 0.0 copy-start.6
  16.3 0.7 copy-done.6
  16.9 61.4 %shard_map.74 = f32[3,320,128]{2,1,0:T(8,128)} custom-call(s32[195]{0:T(256)} %constant.8.clone.plan, f32[328,128]{1,0:T(8,128)} %shard_map.73.refs_0_, f32[328,128]{1,0:T(8,128)} %copy-done, f32[328,128]{1,0:T(8,128)} %copy-done.1, f32[328,128]{1,0:T(8,128)} %copy-done.2, f32[328,128]{1,0:T(8,128)} %copy-done.3, f32[328,128]{1,0:T(8,128)} %copy-done.4, ...), custom_call_target="tpu_custom_call" | custom-call | tf_op jit(solution)/shard_map/pallas_call | solution.py:598
  (2 shorter events, 0.0 us)
Async XLA Ops:
  1.6 8.3 %collective-permute-start = (f32[328,128]{1,0:T(8,128)}, f32[328,128]{1,0:T(8,128)S(1)}, u32[]{:S(2)}, u32[]{:S(2)}) collective-permute-start(f32[328,128]{1,0:T(8,128)} %shard_map.73.refs_0_), channel_id=1, source_target_pairs={{0,1},{1,0},{2,3},{3,2},{4,5},{5,4},{6,7},{7,6},{8,9},{9,8},{10,11... | collective-permute-start | bytes 503816 | tf_op jit(solution)/shard_map/ppermute | solution.py:580
  4.5 9.6 %collective-permute-start.1 = (f32[328,128]{1,0:T(8,128)}, f32[328,128]{1,0:T(8,128)S(1)}, u32[]{:S(2)}, u32[]{:S(2)}) collective-permute-start(f32[328,128]{1,0:T(8,128)} %shard_map.73.refs_0_), channel_id=1, source_target_pairs={{0,2},{1,3},{2,0},{3,1},{4,6},{5,7},{6,4},{7,5},{8,10},{9,11},{10,... | collective-permute-start | bytes 503816 | tf_op jit(solution)/shard_map/ppermute | solution.py:580
  6.1 8.0 %collective-permute-start.2 = (f32[328,128]{1,0:T(8,128)}, f32[328,128]{1,0:T(8,128)S(1)}, u32[]{:S(2)}, u32[]{:S(2)}) collective-permute-start(f32[328,128]{1,0:T(8,128)} %shard_map.73.refs_0_), channel_id=1, source_target_pairs={{0,3},{1,2},{2,1},{3,0},{4,7},{5,6},{6,5},{7,4},{8,11},{9,10},{10,... | collective-permute-start | bytes 503816 | tf_op jit(solution)/shard_map/ppermute | solution.py:580
  6.1 9.4 %collective-permute-start.3 = (f32[328,128]{1,0:T(8,128)}, f32[328,128]{1,0:T(8,128)S(1)}, u32[]{:S(2)}, u32[]{:S(2)}) collective-permute-start(f32[328,128]{1,0:T(8,128)} %shard_map.73.refs_0_), channel_id=1, source_target_pairs={{0,4},{4,0},{1,5},{5,1},{2,6},{6,2},{3,7},{7,3},{8,12},{12,8},{9,1... | collective-permute-start | bytes 503816 | tf_op jit(solution)/shard_map/ppermute | solution.py:581
  7.3 0.8 copy-start.8
  8.0 0.8 copy-start.9
  8.8 0.8 copy-start.7
  9.9 5.8 %copy-start = (f32[328,128]{1,0:T(8,128)}, f32[328,128]{1,0:T(8,128)S(1)}, u32[]{:S(2)}) copy-start(f32[328,128]{1,0:T(8,128)S(1)} %collective-permute-done.refs_1_) | copy-start | bytes 503812
  9.9 5.5 %collective-permute-start.4 = (f32[328,128]{1,0:T(8,128)S(1)}, f32[328,128]{1,0:T(8,128)S(1)}, u32[]{:S(2)}, u32[]{:S(2)}) collective-permute-start(f32[328,128]{1,0:T(8,128)S(1)} %collective-permute-done.refs_1_), channel_id=1, source_target_pairs={{0,4},{4,0},{1,5},{5,1},{2,6},{6,2},{3,7},{7,3},{8,12},{12,8},{9,1... | collective-permute-start | bytes 503816 | tf_op jit(solution)/shard_map/ppermute | solution.py:581
  14.1 1.6 %copy-start.1 = (f32[328,128]{1,0:T(8,128)}, f32[328,128]{1,0:T(8,128)S(1)}, u32[]{:S(2)}) copy-start(f32[328,128]{1,0:T(8,128)S(1)} %collective-permute-done.1.refs_2_) | copy-start | bytes 503812
  14.1 1.4 %collective-permute-start.5 = (f32[328,128]{1,0:T(8,128)S(1)}, f32[328,128]{1,0:T(8,128)S(1)}, u32[]{:S(2)}, u32[]{:S(2)}) collective-permute-start(f32[328,128]{1,0:T(8,128)S(1)} %collective-permute-done.1.refs_2_), channel_id=1, source_target_pairs={{0,4},{4,0},{1,5},{5,1},{2,6},{6,2},{3,7},{7,3},{8,12},{12,8},{9,1... | collective-permute-start | bytes 503816 | tf_op jit(solution)/shard_map/ppermute | solution.py:581
  14.1 1.6 %copy-start.2 = (f32[328,128]{1,0:T(8,128)}, f32[328,128]{1,0:T(8,128)S(1)}, u32[]{:S(2)}) copy-start(f32[328,128]{1,0:T(8,128)S(1)} %collective-permute-done.2.refs_3_) | copy-start | bytes 503812
  14.1 1.6 %collective-permute-start.6 = (f32[328,128]{1,0:T(8,128)S(1)}, f32[328,128]{1,0:T(8,128)S(1)}, u32[]{:S(2)}, u32[]{:S(2)}) collective-permute-start(f32[328,128]{1,0:T(8,128)S(1)} %collective-permute-done.2.refs_3_), channel_id=1, source_target_pairs={{0,4},{4,0},{1,5},{5,1},{2,6},{6,2},{3,7},{7,3},{8,12},{12,8},{9,1... | collective-permute-start | bytes 503816 | tf_op jit(solution)/shard_map/ppermute | solution.py:581
  15.4 0.7 copy-start.3
  15.4 0.7 copy-start.4
  15.5 0.8 copy-start.5
  16.2 0.7 copy-start.6

commit v4 on v3

--- a/solution.py
+++ b/solution.py
@@ -435,8 +435,9 @@
     def kind_5(t):
         def store(row, i, image):
             z = ld(base, row) - image
-            put(zed, row, z)
-            put(vv, row, tab(de, i) * (ld(ss, row) + z) - ld(quad, row), 0, work)
+            rest = tab(de, i) * z - ld(quad, row)
+            put(zed, row, rest)
+            put(vv, row, tab(de, i) * ld(ss, row) + rest, 0, work)
 
         finish(store)
 
@@ -456,7 +457,7 @@
             s = tab(dd, i) * (ld(ss, row, at) + ld(base, row) - image)
             put(ss, row, s, at, SIZE)
             put(vv, row, s, 0, copy)
-            put(vv, row, tab(de, i) * (s + ld(zed, row)) - ld(quad, row), 0, work)
+            put(vv, row, tab(de, i) * s + ld(zed, row), 0, work)
 
         finish(store)
 
@@ -516,8 +517,9 @@
 
         def store(row, i, image):
             z = ld(tt, row, at, SIZE) - image
-            put(gg, row, z, at)
-            put(vv, row, tab(de, i) * (ld(ss, row) + z) - ld(pp, row, at), 0, work)
+            rest = tab(de, i) * z - ld(pp, row, at)
+            put(gg, row, rest, at)
+            put(vv, row, tab(de, i) * ld(ss, row) + rest, 0, work)
 
         finish(store)
 
@@ -528,8 +530,7 @@
         def store(row, i, image):
             s = tab(dd, i) * (ld(tt, row, at) + ld(tt, row, at, SIZE) - image)
             put(tt, row, s, at, SIZE)
-            z = ld(gg, row, later)
-            put(vv, row, tab(de, i) * (s + z) - ld(pp, row, later), 0, work)
+            put(vv, row, tab(de, i) * s + ld(gg, row, later), 0, work)
 
         finish(store)
 

time: 78.7 us -> 78.3 us (level)
  no operation moved by 1% of the time
where the time goes in v4:
time: 78.3 us; the launch traced here: 77.8 us
  Pallas kernels  62.5 us (80%)
  starting transfers between devices  5.53 us (7%)
  local copies, waits for them, and re-layouts  4.97 us (6%)
  waiting for transfers between devices  3.88 us (5%)
  other arithmetic  0.82 us (1%)
    pallas_call x1, Pallas kernels, local(): pl.pallas_call(lambda plan, *refs: whole_grid_kernel(slices, plan, *refs)...  60.9 us
    ppermute x3, starting transfers between devices, local(): near.append(lax.ppermute(block, 'sy', [(i, i ^ k) for i in range(4)]))  4.46 us
    ppermute x3, waiting for transfers between devices, local(): near.append(lax.ppermute(block, 'sy', [(i, i ^ k) for i in range(4)]))  3.59 us
    unnamed x21, local copies, waits for them, and re-layouts  2.32 us
    mul x13, local copies, waits for them, and re-layouts, local(): flux_jacobian[d][None, :, None, :, None] * tables[:, d, None, :, None, :]  1.82 us
    pallas_call x1, Pallas kernels, local(): pl.pallas_call(join_kernel, out_shape=jax.ShapeDtypeStruct((ROWS + 8, 128...  1.59 us
  transfers between devices with their start and end apart: 7, of which 2 were waited for; matrix products, arithmetic and copies ran while one was open for 4% of the time, Pallas kernels for 0%

profile of v4, /device:TPU:0, one launch (start us, length us, event | category | flops | bytes accessed | tf_op | source)
XLA Modules:
  0.0 77.8 jit_solution(3361525489898375735)
XLA Ops:
  0.0 1.6 %shard_map.73.refs_0_ = f32[328,128]{1,0:T(8,128)} custom-call(f32[320,128]{1,0:T(8,128)} %bitcast.12, f32[1,128]{1,0:T(1,128)} %bitcast.14), custom_call_target="tpu_custom_call" | custom-call | tf_op jit(solution)/shard_map/pallas_call | solution.py:573
  1.6 2.9 %collective-permute-start = (f32[328,128]{1,0:T(8,128)}, f32[328,128]{1,0:T(8,128)S(1)}, u32[]{:S(2)}, u32[]{:S(2)}) collective-permute-start(f32[328,128]{1,0:T(8,128)} %shard_map.73.refs_0_), channel_id=1, source_target_pairs={{0,1},{1,0},{2,3},{3,2},{4,5},{5,4},{6,7},{7,6},{8,9},{9,8},{10,11... | collective-permute-start | bytes 503816 | tf_op jit(solution)/shard_map/ppermute | solution.py:581
  4.5 1.5 %collective-permute-start.1 = (f32[328,128]{1,0:T(8,128)}, f32[328,128]{1,0:T(8,128)S(1)}, u32[]{:S(2)}, u32[]{:S(2)}) collective-permute-start(f32[328,128]{1,0:T(8,128)} %shard_map.73.refs_0_), channel_id=1, source_target_pairs={{0,2},{1,3},{2,0},{3,1},{4,6},{5,7},{6,4},{7,5},{8,10},{9,11},{10,... | collective-permute-start | bytes 503816 | tf_op jit(solution)/shard_map/ppermute | solution.py:581
  6.1 0.0 collective-permute-start.2
  6.1 0.0 collective-permute-start.3
  6.1 0.8 %fusion = (f32[1,5,5]{2,0,1:T(1,128)S(1)}, f32[1,5,5]{2,0,1:T(1,128)S(1)}, f32[1,5,5]{2,0,1:T(1,128)S(1)}) fusion(f32[3,5,5]{2,0,1:T(4,128)} %param.9), kind=kLoop, calls=%fused_computation.4 | loop fusion | bytes 600 | tf_op jit(solution)/shard_map/slice | solution.py:590
  6.9 0.1 mul.81
  7.0 0.1 mul.82
  7.1 0.1 mul.89
  7.3 0.0 copy-start.8
  7.3 0.1 mul.90
  7.4 0.1 mul.73
  7.5 0.1 mul.74
  7.7 0.4 copy-done.8
  8.0 0.0 copy-start.9
  8.0 0.1 mul.77
  8.1 0.3 mul.78
  8.4 0.4 copy-done.9
  8.8 0.0 copy-start.7
  8.8 0.1 mul.85
  8.9 0.3 mul.86
  9.1 0.4 copy-done.7
  9.5 0.1 mul.93
  9.6 0.3 mul.94
  9.9 0.0 collective-permute-done.refs_1_
  9.9 0.0 copy-start
  9.9 0.6 collective-permute-start.4
  10.5 3.6 %collective-permute-done.1.refs_2_ = f32[328,128]{1,0:T(8,128)S(1)} collective-permute-done((f32[328,128]{1,0:T(8,128)}, f32[328,128]{1,0:T(8,128)S(1)}, u32[]{:S(2)}, u32[]{:S(2)}) %collective-permute-start.1) | collective-permute-done | bytes 167968 | tf_op jit(solution)/shard_map/ppermute | solution.py:581
  14.1 0.0 copy-start.1
  14.1 0.0 collective-permute-start.5
  14.1 0.0 collective-permute-done.2.refs_3_
  14.1 0.0 copy-start.2
  14.1 0.5 collective-permute-start.6
  14.6 0.8 %multiply_add_fusion.refs_8_ = f32[2,160,160]{2,1,0:T(8,128)} fusion(f32[2,160,160]{2,1,0:T(8,128)S(1)} %mul.94, f32[2,160,160]{2,1,0:T(8,128)S(1)} %mul.86, f32[2,160,160]{2,1,0:T(8,128)S(1)} %mul.78, f32[160,160]{1,0:T(8,128)S(1)} %mul.90, f32[160,160]{1,0:T(8,128)S(1)} %mul.82, f32[160,160]{1,0:T(8,128)S(1)} %mul.74), kind=kLoop, calls=%fused_computation | loop fusion | flops 256000 | bytes 1126400 | tf_op jit(solution)/shard_map/add | solution.py:589
  15.4 0.0 collective-permute-done.3.refs_4_
  15.4 0.0 copy-start.3
  15.4 0.0 collective-permute-done.4.refs_5_
  15.4 0.0 copy-start.4
  15.4 0.0 collective-permute-done.5.refs_6_
  15.5 0.0 copy-start.5
  15.5 0.2 collective-permute-done.6.refs_7_
  15.7 0.0 copy-done
  15.7 0.0 copy-done.1
  15.7 0.0 copy-done.2
  15.7 0.4 copy-done.3
  16.1 0.1 copy-done.4
  16.2 0.1 copy-done.5
  16.2 0.0 copy-start.6
  16.3 0.7 copy-done.6
  16.9 60.9 %shard_map.74 = f32[3,320,128]{2,1,0:T(8,128)} custom-call(s32[195]{0:T(256)} %constant.8.clone.plan, f32[328,128]{1,0:T(8,128)} %shard_map.73.refs_0_, f32[328,128]{1,0:T(8,128)} %copy-done, f32[328,128]{1,0:T(8,128)} %copy-done.1, f32[328,128]{1,0:T(8,128)} %copy-done.2, f32[328,128]{1,0:T(8,128)} %copy-done.3, f32[328,128]{1,0:T(8,128)} %copy-done.4, ...), custom_call_target="tpu_custom_call" | custom-call | tf_op jit(solution)/shard_map/pallas_call | solution.py:599
  (2 shorter events, 0.0 us)
Async XLA Ops:
  1.6 8.3 %collective-permute-start = (f32[328,128]{1,0:T(8,128)}, f32[328,128]{1,0:T(8,128)S(1)}, u32[]{:S(2)}, u32[]{:S(2)}) collective-permute-start(f32[328,128]{1,0:T(8,128)} %shard_map.73.refs_0_), channel_id=1, source_target_pairs={{0,1},{1,0},{2,3},{3,2},{4,5},{5,4},{6,7},{7,6},{8,9},{9,8},{10,11... | collective-permute-start | bytes 503816 | tf_op jit(solution)/shard_map/ppermute | solution.py:581
  4.5 9.6 %collective-permute-start.1 = (f32[328,128]{1,0:T(8,128)}, f32[328,128]{1,0:T(8,128)S(1)}, u32[]{:S(2)}, u32[]{:S(2)}) collective-permute-start(f32[328,128]{1,0:T(8,128)} %shard_map.73.refs_0_), channel_id=1, source_target_pairs={{0,2},{1,3},{2,0},{3,1},{4,6},{5,7},{6,4},{7,5},{8,10},{9,11},{10,... | collective-permute-start | bytes 503816 | tf_op jit(solution)/shard_map/ppermute | solution.py:581
  6.1 8.0 %collective-permute-start.2 = (f32[328,128]{1,0:T(8,128)}, f32[328,128]{1,0:T(8,128)S(1)}, u32[]{:S(2)}, u32[]{:S(2)}) collective-permute-start(f32[328,128]{1,0:T(8,128)} %shard_map.73.refs_0_), channel_id=1, source_target_pairs={{0,3},{1,2},{2,1},{3,0},{4,7},{5,6},{6,5},{7,4},{8,11},{9,10},{10,... | collective-permute-start | bytes 503816 | tf_op jit(solution)/shard_map/ppermute | solution.py:581
  6.1 9.4 %collective-permute-start.3 = (f32[328,128]{1,0:T(8,128)}, f32[328,128]{1,0:T(8,128)S(1)}, u32[]{:S(2)}, u32[]{:S(2)}) collective-permute-start(f32[328,128]{1,0:T(8,128)} %shard_map.73.refs_0_), channel_id=1, source_target_pairs={{0,4},{4,0},{1,5},{5,1},{2,6},{6,2},{3,7},{7,3},{8,12},{12,8},{9,1... | collective-permute-start | bytes 503816 | tf_op jit(solution)/shard_map/ppermute | solution.py:582
  7.3 0.8 copy-start.8
  8.0 0.8 copy-start.9
  8.8 0.8 copy-start.7
  9.9 5.8 %copy-start = (f32[328,128]{1,0:T(8,128)}, f32[328,128]{1,0:T(8,128)S(1)}, u32[]{:S(2)}) copy-start(f32[328,128]{1,0:T(8,128)S(1)} %collective-permute-done.refs_1_) | copy-start | bytes 503812
  9.9 5.5 %collective-permute-start.4 = (f32[328,128]{1,0:T(8,128)S(1)}, f32[328,128]{1,0:T(8,128)S(1)}, u32[]{:S(2)}, u32[]{:S(2)}) collective-permute-start(f32[328,128]{1,0:T(8,128)S(1)} %collective-permute-done.refs_1_), channel_id=1, source_target_pairs={{0,4},{4,0},{1,5},{5,1},{2,6},{6,2},{3,7},{7,3},{8,12},{12,8},{9,1... | collective-permute-start | bytes 503816 | tf_op jit(solution)/shard_map/ppermute | solution.py:582
  14.1 1.6 %copy-start.1 = (f32[328,128]{1,0:T(8,128)}, f32[328,128]{1,0:T(8,128)S(1)}, u32[]{:S(2)}) copy-start(f32[328,128]{1,0:T(8,128)S(1)} %collective-permute-done.1.refs_2_) | copy-start | bytes 503812
  14.1 1.4 %collective-permute-start.5 = (f32[328,128]{1,0:T(8,128)S(1)}, f32[328,128]{1,0:T(8,128)S(1)}, u32[]{:S(2)}, u32[]{:S(2)}) collective-permute-start(f32[328,128]{1,0:T(8,128)S(1)} %collective-permute-done.1.refs_2_), channel_id=1, source_target_pairs={{0,4},{4,0},{1,5},{5,1},{2,6},{6,2},{3,7},{7,3},{8,12},{12,8},{9,1... | collective-permute-start | bytes 503816 | tf_op jit(solution)/shard_map/ppermute | solution.py:582
  14.1 1.6 %copy-start.2 = (f32[328,128]{1,0:T(8,128)}, f32[328,128]{1,0:T(8,128)S(1)}, u32[]{:S(2)}) copy-start(f32[328,128]{1,0:T(8,128)S(1)} %collective-permute-done.2.refs_3_) | copy-start | bytes 503812
  14.1 1.6 %collective-permute-start.6 = (f32[328,128]{1,0:T(8,128)S(1)}, f32[328,128]{1,0:T(8,128)S(1)}, u32[]{:S(2)}, u32[]{:S(2)}) collective-permute-start(f32[328,128]{1,0:T(8,128)S(1)} %collective-permute-done.2.refs_3_), channel_id=1, source_target_pairs={{0,4},{4,0},{1,5},{5,1},{2,6},{6,2},{3,7},{7,3},{8,12},{12,8},{9,1... | collective-permute-start | bytes 503816 | tf_op jit(solution)/shard_map/ppermute | solution.py:582
  15.4 0.7 copy-start.3
  15.4 0.7 copy-start.4
  15.5 0.8 copy-start.5
  16.2 0.7 copy-start.6
